TPU v7x, 256 devices: a whole 4x4x8 slice. The times are simulated.
256 devices in a mesh: row: 16 (over x, y_hi, core), col: 16 (over z, y_lo).
Axes of the slice: x: 4, y: 4 (y_hi: 2, y_lo: 2; y = y_hi * 2 + y_lo), z: 8, core: 2. Of those that a mesh axis runs over, the one named last changes fastest.
Arguments:
- sequence: bfloat16 [128, 256, 768], P('row', 'col'), may hold values from -6 to 6
- conv_weights: float32 [3, 2304], replicated, may hold values from -3.5 to 3.5
- cotangent: bfloat16 [128, 256, 768], P('row', 'col'), may hold values from -6 to 6
- filter_re: bfloat16 [128, 768, 256], P('col', 'row'), may hold values from -6 to 6
- filter_im: bfloat16 [128, 768, 256], P('col', 'row'), may hold values from -6 to 6
Outputs:
- mixed: bfloat16 [128, 256, 768], P('row', 'col')
- input_grad: bfloat16 [128, 256, 768], P('row', 'col')
- filter_grad_re: float32 [128, 768, 256], P('col', 'row')
- filter_grad_im: float32 [128, 768, 256], P('col', 'row')
- conv_weight_grad: float32 [3, 2304], replicated
All inputs are finite; a program needn't handle non-finite values.
Results may differ from a plain program's by a relative error of at most 0.0091.
Values may be sent and summed in bfloat16 or wider, within the bound.
A program may use at most 64 MiB of HBM per device.

v0:
```python
import math

import jax
import jax.numpy as jnp
from jax import lax
from jax.sharding import PartitionSpec as P


def from_behind(shard, axis, by):
    peers = lax.axis_size(axis)
    return lax.ppermute(shard, axis, [(i, (i + by) % peers) for i in range(peers)])


def from_behind_2(shard, axis, by):
    peers = lax.axis_size(axis)
    pairs = [(i, i + by) for i in range(peers) if 0 <= i + by < peers]
    return lax.ppermute(shard, axis, pairs)


def dft_tables(length):
    index_row = jnp.arange(length, dtype=jnp.int32)
    product = index_row[:, None] * index_row[None, :] % length
    angles = product.astype(jnp.float32) * (2.0 * math.pi / length)
    return (jnp.cos(angles).astype(jnp.bfloat16), jnp.sin(angles).astype(jnp.bfloat16))


def phase_table(first_index, second_index, seq_total):
    product = first_index[:, None] * second_index[None, :] % seq_total
    angles = product.astype(jnp.float32) * (2.0 * math.pi / seq_total)
    return (jnp.cos(angles), jnp.sin(angles))


def per_device(sequence, conv_weights, cotangent, filter_re, filter_im):
    row_count, col_count, channels = sequence.shape
    row_devices = lax.axis_size("row")
    col_devices = lax.axis_size("col")
    first_len = row_count * row_devices
    second_len = col_count * col_devices
    seq_total = first_len * second_len
    spec_rows = first_len // col_devices
    chan_local = channels // row_devices
    col_place = lax.axis_index("col")
    cos_first, sin_first = dft_tables(first_len)
    cos_second, sin_second = dft_tables(second_len)
    fwd_cos, fwd_sin = phase_table(
        jnp.arange(first_len, dtype=jnp.int32),
        col_place * col_count + jnp.arange(col_count, dtype=jnp.int32),
        seq_total,
    )
    inv_cos, inv_sin = phase_table(
        col_place * spec_rows + jnp.arange(spec_rows, dtype=jnp.int32),
        jnp.arange(second_len, dtype=jnp.int32),
        seq_total,
    )
    fwd_cos = jnp.repeat(fwd_cos, chan_local, axis=1)[None]
    fwd_sin = jnp.repeat(fwd_sin, chan_local, axis=1)[None]
    inv_cos = inv_cos[None, :, :, None]
    inv_sin = inv_sin[None, :, :, None]

    def first_section(panels):
        lead, length, items, width = panels.shape
        flat = panels.reshape(lead, length, items * width)
        real_part = jnp.stack([jnp.dot(cos_first, flat[0], preferred_element_type=jnp.float32)])
        imag_part = jnp.stack([-jnp.dot(sin_first, flat[0], preferred_element_type=jnp.float32)])
        return (real_part, imag_part)

    def second_section(panels):
        part_re, part_im = panels
        lead = part_re.shape[0]
        rows_here = part_re.shape[1]
        part_re = part_re.reshape(lead, rows_here, second_len, chan_local)
        part_im = part_im.reshape(lead, rows_here, second_len, chan_local)
        out_re = jnp.einsum(
            "mknd,nj->mkdj", part_re, cos_second, preferred_element_type=jnp.float32
        ) + jnp.einsum("mknd,nj->mkdj", part_im, sin_second, preferred_element_type=jnp.float32)
        out_im = jnp.einsum(
            "mknd,nj->mkdj", part_im, cos_second, preferred_element_type=jnp.float32
        ) - jnp.einsum("mknd,nj->mkdj", part_re, sin_second, preferred_element_type=jnp.float32)
        return (out_re, out_im)

    def last_section(panels):
        part_re, part_im = panels
        lead = part_re.shape[0]
        return jnp.stack(
            [
                jnp.dot(cos_first, part_re[0], preferred_element_type=jnp.float32)
                - jnp.dot(sin_first, part_im[0], preferred_element_type=jnp.float32)
            ]
        )

    def spectrum(fields):
        first_re, first_im = first_section(
            lax.all_to_all(fields, "row", split_axis=3, concat_axis=1, tiled=True)
        )
        twisted_re = (first_re * fwd_cos + first_im * fwd_sin).astype(jnp.bfloat16)
        twisted_im = (first_im * fwd_cos - first_re * fwd_sin).astype(jnp.bfloat16)
        return second_section(
            (
                lax.all_to_all(twisted_re, "col", split_axis=1, concat_axis=2, tiled=True),
                lax.all_to_all(twisted_im, "col", split_axis=1, concat_axis=2, tiled=True),
            )
        )

    def restore(spec_re, spec_im):
        lead = spec_re.shape[0]
        inner_re = jnp.einsum(
            "mkdj,jn->mknd", spec_re, cos_second, preferred_element_type=jnp.float32
        ) - jnp.einsum("mkdj,jn->mknd", spec_im, sin_second, preferred_element_type=jnp.float32)
        inner_im = jnp.einsum(
            "mkdj,jn->mknd", spec_im, cos_second, preferred_element_type=jnp.float32
        ) + jnp.einsum("mkdj,jn->mknd", spec_re, sin_second, preferred_element_type=jnp.float32)
        turned_re = (
            (inner_re * inv_cos - inner_im * inv_sin)
            .astype(jnp.bfloat16)
            .reshape(lead, spec_rows, second_len * chan_local)
        )
        turned_im = (
            (inner_im * inv_cos + inner_re * inv_sin)
            .astype(jnp.bfloat16)
            .reshape(lead, spec_rows, second_len * chan_local)
        )
        summed = last_section(
            (
                lax.all_to_all(turned_re, "col", split_axis=2, concat_axis=1, tiled=True),
                lax.all_to_all(turned_im, "col", split_axis=2, concat_axis=1, tiled=True),
            )
        )
        scaled = (
            (summed / seq_total)
            .astype(jnp.bfloat16)
            .reshape(lead, first_len, col_count, chan_local)
        )
        return lax.all_to_all(scaled, "row", split_axis=1, concat_axis=3, tiled=True)

    left_cols = from_behind(sequence[:, col_count - 2 :, :], "col", 1)
    corner = from_behind_2(left_cols[row_count - 1 :], "row", 1)
    wrapped = jnp.concatenate([corner, left_cols[: row_count - 1]], 0)
    left_cols = jnp.where(col_place == 0, wrapped, left_cols)
    padded = jnp.concatenate([left_cols, sequence], 1).astype(jnp.float32)
    previous = [padded[:, 2 - offset : 2 - offset + col_count] for offset in range(3)]
    tap_weights = conv_weights.reshape(3, 3, channels)
    streams = []
    for stream in range(3):
        total_sum = tap_weights[0, stream] * previous[0]
        total_sum = total_sum + tap_weights[1, stream] * previous[1]
        total_sum = total_sum + tap_weights[2, stream] * previous[2]
        streams.append(total_sum)
    stream_a, stream_b, stream_c = streams
    gated = (stream_a * stream_b).astype(jnp.bfloat16)
    grad_f = cotangent.astype(jnp.float32)
    grad_gate = (grad_f * stream_c).astype(jnp.bfloat16)
    first_re, first_im = spectrum(gated[None])
    spec_re, spec_im = (first_re[0], first_im[0])
    prod_re = (spec_re * filter_re - spec_im * filter_im).astype(jnp.bfloat16)
    prod_im = (spec_re * filter_im + spec_im * filter_re).astype(jnp.bfloat16)
    filtered = restore(prod_re[None], prod_im[None])[0]
    second_re, second_im = spectrum(grad_gate[None])
    gspec_re, gspec_im = (second_re[0], second_im[0])
    back_re = (gspec_re * filter_re + gspec_im * filter_im).astype(jnp.bfloat16)
    back_im = (gspec_im * filter_re - gspec_re * filter_im).astype(jnp.bfloat16)
    grad_filtered = restore(back_re[None], back_im[None])[0]
    fgrad_re = (spec_re * gspec_re + spec_im * gspec_im) / seq_total
    fgrad_im = (spec_re * gspec_im - spec_im * gspec_re) / seq_total
    filtered_f = filtered.astype(jnp.float32)
    mixed = (stream_c * filtered_f).astype(jnp.bfloat16)
    grad_filt_f = grad_filtered.astype(jnp.float32)
    stacked = jnp.concatenate(
        [grad_filt_f * stream_b, grad_filt_f * stream_a, grad_f * filtered_f], 2
    ).astype(jnp.bfloat16)
    right_cols = from_behind(stacked[:, :2, :], "col", -1)
    corner_next = from_behind_2(right_cols[:1], "row", -1)
    wrapped_next = jnp.concatenate([right_cols[1:], corner_next], 0)
    right_cols = jnp.where(col_place == col_devices - 1, wrapped_next, right_cols)
    ahead = jnp.concatenate([stacked, right_cols], 1).astype(jnp.float32)
    input_acc = jnp.zeros((row_count, col_count, channels), jnp.float32)
    for offset in range(3):
        shifted = ahead[:, offset : offset + col_count].reshape(row_count, col_count, 3, channels)
        for stream in range(3):
            input_acc = input_acc + tap_weights[offset, stream] * shifted[:, :, stream]
    input_grad = input_acc.astype(jnp.bfloat16)
    own_grads = ahead[:, :col_count].reshape(row_count, col_count, 3, channels)
    weight_rows = []
    for offset in range(3):
        weight_rows.append(jnp.sum(previous[offset][:, :, None, :] * own_grads, axis=(0, 1)))
    local_terms = jnp.stack(weight_rows).reshape(3, 3 * channels)
    weight_grad = lax.psum(local_terms, ("row", "col")) / math.sqrt(seq_total)
    return (mixed, input_grad, fgrad_re, fgrad_im, weight_grad)


def solution(mesh):
    return jax.shard_map(
        per_device,
        mesh=mesh,
        in_specs=(
            P("row", "col", None),
            P(),
            P("row", "col", None),
            P("col", "row", None),
            P("col", "row", None),
        ),
        out_specs=(
            P("row", "col", None),
            P("row", "col", None),
            P("col", "row", None),
            P("col", "row", None),
            P(),
        ),
        check_vma=False,
    )
```

profile of v0, /device:TPU:1, one launch (start us, length us, event | category | flops | bytes accessed | tf_op | source)
XLA Modules:
  0.0 745.3 jit_solution(11902994871313481716)
XLA Ops:
  1.6 2.2 collective-permute-start
  5.2 5.0 collective-permute-done
  10.3 5.9 collective-permute-start.1
  18.0 2.2 fusion.47
  21.2 2.3 reshape.292
  23.6 7.9 %all-to-all-start.6 = ((bf16[16,2,3072]{2,1,0:T(2,128)(2,1)}), bf16[16,2,3072]{2,1,0:T(2,128)(2,1)S(1)}, u32[]{:S(2)}, u32[]{:S(2)}) async-start(bf16[16,2,3072]{2,1,0:T(2,128)(2,1)} %reshape.292), calls=%async_computation.6 | async-start | bytes 393216 | tf_op jit(solution)/shard_map/all_to_all | solution.py:93
  32.0 7.8 %all-to-all-done.6 = bf16[16,2,3072]{2,1,0:T(2,128)(2,1)S(1)} async-done(((bf16[16,2,3072]{2,1,0:T(2,128)(2,1)}), bf16[16,2,3072]{2,1,0:T(2,128)(2,1)S(1)}, u32[]{:S(2)}, u32[]{:S(2)}) %all-to-all-start.6) | async-done | bytes 196640 | tf_op jit(solution)/shard_map/all_to_all | solution.py:93
  44.0 1.7 reduce.21
  46.5 5.8 all-to-all-start.8
  52.7 1.7 reduce.22
  55.1 6.8 all-to-all-done.8
  61.9 3.7 all-to-all-start.7
  67.9 6.8 all-to-all-done.7
  76.4 2.2 fusion.74
  78.6 2.2 convolution_subtract_fusion.4
  80.8 2.0 fusion.15
  88.6 10.2 %copy.229 = bf16[1,8,12288]{1,0,2:T(2,128)(2,1)} copy(bf16[1,8,12288]{2,1,0:T(8,128)(2,1)S(1)} %reshape.259) | data formatting | bytes 393216 | tf_op jit(solution)/shard_map/reshape | solution.py:115
  98.9 68.6 %reduce.23 = bf16[12288,8]{1,0:T(8,128)(2,1)} reduce(bf16[12288,1,8]{2,1,0:T(2,128)(2,1)} %bitcast.291, bf16[]{:T(256)} %broadcast.195), dimensions={1}, to_apply=%bitcast.236.reduce_sub_computation | reduce | bytes 393218
  167.5 5.6 reshape.298
  173.1 3.7 all-to-all-start.9
  177.8 9.8 %copy.233 = bf16[1,8,12288]{1,0,2:T(2,128)(2,1)} copy(bf16[1,8,12288]{2,1,0:T(8,128)(2,1)S(1)} %reshape.260) | data formatting | bytes 393216 | tf_op jit(solution)/shard_map/reshape | solution.py:120
  187.7 68.6 %reduce.24 = bf16[12288,8]{1,0:T(8,128)(2,1)} reduce(bf16[12288,1,8]{2,1,0:T(2,128)(2,1)} %bitcast.292, bf16[]{:T(256)} %broadcast.195), dimensions={1}, to_apply=%bitcast.238.reduce_sub_computation | reduce | bytes 393218
  256.3 5.6 reshape.300
  261.9 7.6 %all-to-all-start.10 = ((bf16[16,2,3072]{2,1,0:T(2,128)(2,1)}), bf16[16,2,3072]{2,1,0:T(2,128)(2,1)S(1)}, u32[]{:S(2)}, u32[]{:S(2)}) async-start(bf16[16,2,3072]{2,1,0:T(2,128)(2,1)} %reshape.300), calls=%async_computation.10 | async-start | bytes 393216 | tf_op jit(solution)/shard_map/all_to_all | solution.py:125
  269.5 10.5 %reshape.299 = bf16[12288,1,8]{2,1,0:T(2,128)(2,1)} reshape(bf16[16,2,3072]{2,1,0:T(2,128)(2,1)S(1)} %all-to-all-done.9) | data formatting | bytes 393216
  279.9 11.3 %copy.230 = bf16[1,8,12288]{2,1,0:T(8,128)(2,1)S(1)} copy(bf16[1,8,12288]{1,0,2:T(2,128)(2,1)} %bitcast.293) | data formatting | bytes 393216 | tf_op jit(solution)/shard_map/all_to_all | solution.py:124
  291.8 10.5 %reshape.301 = bf16[12288,1,8]{2,1,0:T(2,128)(2,1)} reshape(bf16[16,2,3072]{2,1,0:T(2,128)(2,1)S(1)} %all-to-all-done.10) | data formatting | bytes 393216
  302.2 11.3 %copy.234 = bf16[1,8,12288]{2,1,0:T(8,128)(2,1)S(1)} copy(bf16[1,8,12288]{1,0,2:T(2,128)(2,1)} %bitcast.294) | data formatting | bytes 393216 | tf_op jit(solution)/shard_map/all_to_all | solution.py:125
  315.4 14.9 %all_to_all.168 = bf16[16,2,3072]{2,1,0:T(2,128)(2,1)S(1)} all-to-all(bf16[16,2,3072]{2,1,0:T(2,128)(2,1)S(1)} %reshape.302), channel_id=1, replica_groups=mesh['row'=16,'col'=16] {'row'}, dimensions={0} | all-to-all | bytes 393216 | tf_op jit(solution)/shard_map/all_to_all | solution.py:133
  333.5 1.7 reshape.280
  335.1 11.2 %all_to_all.169 = bf16[16,2,3072]{2,1,0:T(2,128)(2,1)S(1)} all-to-all(bf16[16,2,3072]{2,1,0:T(2,128)(2,1)S(1)} %reshape.280), channel_id=1, replica_groups=mesh['row'=16,'col'=16] {'row'}, dimensions={0} | all-to-all | bytes 393216 | tf_op jit(solution)/shard_map/all_to_all | solution.py:93
  350.0 1.7 reduce.25
  352.5 7.8 %all-to-all-start.1 = ((bf16[16,2,3072]{2,1,0:T(2,128)(2,1)}), bf16[16,2,3072]{2,1,0:T(2,128)(2,1)S(1)}, u32[]{:S(2)}, u32[]{:S(2)}) async-start(bf16[16,2,3072]{2,1,0:T(2,128)(2,1)} %reshape.284), calls=%async_computation.1 | async-start | bytes 393216 | tf_op jit(solution)/shard_map/all_to_all | solution.py:99
  360.6 1.7 reduce.26
  363.1 6.8 all-to-all-done.1
  369.9 3.9 all-to-all-start.2
  374.7 1.9 fusion.82
  376.6 6.2 all-to-all-done.2
  384.9 2.2 convolution_add_fusion.3
  387.1 2.2 subtract_multiply_fusion
  392.9 1.9 add_convert_fusion.2
  395.8 10.0 %copy.203 = bf16[1,8,12288]{1,0,2:T(2,128)(2,1)} copy(bf16[1,8,12288]{2,1,0:T(8,128)(2,1)S(1)} %reshape.254) | data formatting | bytes 393216 | tf_op jit(solution)/shard_map/reshape | solution.py:115
  405.8 66.9 %reduce.27 = bf16[12288,8]{1,0:T(8,128)(2,1)S(1)} reduce(bf16[12288,1,8]{2,1,0:T(2,128)(2,1)} %bitcast.295, bf16[]{:T(256)} %broadcast.195), dimensions={1}, to_apply=%bitcast.224.reduce_sub_computation | reduce | bytes 393218
  472.7 4.0 reshape.286
  476.7 4.4 all-to-all-start.3
  483.1 9.8 %copy.207 = bf16[1,8,12288]{1,0,2:T(2,128)(2,1)} copy(bf16[1,8,12288]{2,1,0:T(8,128)(2,1)S(1)} %reshape.255) | data formatting | bytes 393216 | tf_op jit(solution)/shard_map/reshape | solution.py:120
  493.0 66.9 %reduce.28 = bf16[12288,8]{1,0:T(8,128)(2,1)S(1)} reduce(bf16[12288,1,8]{2,1,0:T(2,128)(2,1)} %bitcast.290, bf16[]{:T(256)} %broadcast.195), dimensions={1}, to_apply=%bitcast.226.reduce_sub_computation | reduce | bytes 393218
  559.9 4.0 reshape.288
  563.9 7.8 %all-to-all-start.4 = ((bf16[16,2,3072]{2,1,0:T(2,128)(2,1)}), bf16[16,2,3072]{2,1,0:T(2,128)(2,1)S(1)}, u32[]{:S(2)}, u32[]{:S(2)}) async-start(bf16[16,2,3072]{2,1,0:T(2,128)(2,1)} %reshape.288), calls=%async_computation.4 | async-start | bytes 393216 | tf_op jit(solution)/shard_map/all_to_all | solution.py:125
  571.7 11.7 %reshape.287 = bf16[12288,1,8]{2,1,0:T(2,128)(2,1)} reshape(bf16[16,2,3072]{2,1,0:T(2,128)(2,1)} %all-to-all-done.3) | data formatting | bytes 393216
  583.4 11.3 %copy.204 = bf16[1,8,12288]{2,1,0:T(8,128)(2,1)S(1)} copy(bf16[1,8,12288]{1,0,2:T(2,128)(2,1)} %bitcast.296) | data formatting | bytes 393216 | tf_op jit(solution)/shard_map/all_to_all | solution.py:124
  595.3 10.5 %reshape.289 = bf16[12288,1,8]{2,1,0:T(2,128)(2,1)} reshape(bf16[16,2,3072]{2,1,0:T(2,128)(2,1)S(1)} %all-to-all-done.4) | data formatting | bytes 393216
  605.7 11.3 %copy.208 = bf16[1,8,12288]{2,1,0:T(8,128)(2,1)S(1)} copy(bf16[1,8,12288]{1,0,2:T(2,128)(2,1)} %bitcast.297) | data formatting | bytes 393216 | tf_op jit(solution)/shard_map/all_to_all | solution.py:125
  619.0 15.4 %all_to_all.170 = bf16[16,2,3072]{2,1,0:T(2,128)(2,1)S(1)} all-to-all(bf16[16,2,3072]{2,1,0:T(2,128)(2,1)S(1)} %reshape.290), channel_id=1, replica_groups=mesh['row'=16,'col'=16] {'row'}, dimensions={0} | all-to-all | bytes 393216 | tf_op jit(solution)/shard_map/all_to_all | solution.py:133
  636.9 3.4 collective-permute-start.2
  641.7 3.2 collective-permute-start.3
  647.3 1.7 mul.685
  650.3 1.7 mul.688
  653.5 2.5 multiply_reduce_fusion.2
  656.1 1.7 reshape.264
  657.8 1.9 fusion.206
  660.5 1.7 reshape.263
  664.3 75.8 %psum.7 = f32[3,2304]{1,0:T(4,128)} all-reduce(f32[3,2304]{1,0:T(4,128)} %pad_maximum_fusion.2), channel_id=1, replica_groups=mesh['row'=16,'col'=16] {'row','col'}, use_global_device_ids=true, to_apply=%region_3.4 | all-reduce | flops 6912 | bytes 55296 | tf_op jit(solution)/shard_map/psum | solution.py:186
  741.5 2.2 fusion.204
  (185 shorter events, 59.4 us)
Async XLA Ops:
  1.6 8.7 %collective-permute-start = (bf16[8,2,768]{2,1,0:T(2,128)(2,1)S(1)}, bf16[8,2,768]{2,1,0:T(2,128)(2,1)S(1)}, u32[]{:S(2)}, u32[]{:S(2)}) collective-permute-start(bf16[8,2,768]{2,1,0:T(2,128)(2,1)S(1)} %slice.101), channel_id=1, source_target_pairs={{0,1},{1,2},{2,3},{3,4},{4,5},{5,6},{6,7},{7,8},{8,9},{9,10},{10,1... | collective-permute-start | bytes 73736 | tf_op jit(solution)/shard_map/ppermute | solution.py:11
  5.2 15.0 %copy-start.24 = (f32[768]{0:T(1024)}, f32[768]{0:T(1024)S(1)}, u32[]{:S(2)}) copy-start(f32[768]{0:T(1024)S(1)} %get-tuple-element.14) | copy-start | bytes 9220
  5.2 15.0 %copy-start.26 = (f32[768]{0:T(1024)}, f32[768]{0:T(1024)S(1)}, u32[]{:S(2)}) copy-start(f32[768]{0:T(1024)S(1)} %get-tuple-element.15) | copy-start | bytes 9220
  5.2 15.0 %copy-start.28 = (f32[768]{0:T(1024)}, f32[768]{0:T(1024)S(1)}, u32[]{:S(2)}) copy-start(f32[768]{0:T(1024)S(1)} %get-tuple-element.16) | copy-start | bytes 9220
  5.2 326.9 %copy-start.14 = (f32[768]{0:T(1024)}, f32[768]{0:T(1024)S(1)}, u32[]{:S(2)}) copy-start(f32[768]{0:T(1024)S(1)} %get-tuple-element.9) | copy-start | bytes 9220
  5.2 326.9 %copy-start.16 = (f32[768]{0:T(1024)}, f32[768]{0:T(1024)S(1)}, u32[]{:S(2)}) copy-start(f32[768]{0:T(1024)S(1)} %get-tuple-element.10) | copy-start | bytes 9220
  5.2 326.9 %copy-start.18 = (f32[768]{0:T(1024)}, f32[768]{0:T(1024)S(1)}, u32[]{:S(2)}) copy-start(f32[768]{0:T(1024)S(1)} %get-tuple-element.11) | copy-start | bytes 9220
  10.3 6.7 collective-permute-start.1
  23.6 16.2 %all-to-all-start.6 = ((bf16[16,2,3072]{2,1,0:T(2,128)(2,1)}), bf16[16,2,3072]{2,1,0:T(2,128)(2,1)S(1)}, u32[]{:S(2)}, u32[]{:S(2)}) async-start(bf16[16,2,3072]{2,1,0:T(2,128)(2,1)} %reshape.292), calls=%async_computation.6 | async-start | bytes 393216 | tf_op jit(solution)/shard_map/all_to_all | solution.py:93
  46.5 15.4 %all-to-all-start.8 = ((bf16[16,2,3072]{2,1,0:T(2,128)(2,1)}), bf16[16,2,3072]{2,1,0:T(2,128)(2,1)S(1)}, u32[]{:S(2)}, u32[]{:S(2)}) async-start(bf16[16,2,3072]{2,1,0:T(2,128)(2,1)} %reshape.294), calls=%async_computation.8 | async-start | bytes 393216 | tf_op jit(solution)/shard_map/all_to_all | solution.py:100
  61.9 12.8 %all-to-all-start.7 = ((bf16[16,2,3072]{2,1,0:T(2,128)(2,1)}), bf16[16,2,3072]{2,1,0:T(2,128)(2,1)S(1)}, u32[]{:S(2)}, u32[]{:S(2)}) async-start(bf16[16,2,3072]{2,1,0:T(2,128)(2,1)} %reshape.296), calls=%async_computation.7 | async-start | bytes 393216 | tf_op jit(solution)/shard_map/all_to_all | solution.py:99
  65.8 20.5 %copy-start.30 = (f32[8,256]{1,0:T(8,128)}, f32[8,256]{1,0:T(8,128)S(1)}, u32[]{:S(2)}) copy-start(f32[8,256]{1,0:T(8,128)S(1)} %get-tuple-element.58) | copy-start | bytes 24580
  65.8 20.5 %copy-start.32 = (f32[8,256]{1,0:T(8,128)}, f32[8,256]{1,0:T(8,128)S(1)}, u32[]{:S(2)}) copy-start(f32[8,256]{1,0:T(8,128)S(1)} %get-tuple-element.59) | copy-start | bytes 24580
  74.9 5.9 copy-start.10
  74.9 5.9 copy-start.11
  80.8 3.2 copy-start.3
  173.1 88.8 %all-to-all-start.9 = ((bf16[16,2,3072]{2,1,0:T(2,128)(2,1)}), bf16[16,2,3072]{2,1,0:T(2,128)(2,1)S(1)}, u32[]{:S(2)}, u32[]{:S(2)}) async-start(bf16[16,2,3072]{2,1,0:T(2,128)(2,1)} %reshape.298), calls=%async_computation.9 | async-start | bytes 393216 | tf_op jit(solution)/shard_map/all_to_all | solution.py:124
  261.9 29.9 %all-to-all-start.10 = ((bf16[16,2,3072]{2,1,0:T(2,128)(2,1)}), bf16[16,2,3072]{2,1,0:T(2,128)(2,1)S(1)}, u32[]{:S(2)}, u32[]{:S(2)}) async-start(bf16[16,2,3072]{2,1,0:T(2,128)(2,1)} %reshape.300), calls=%async_computation.10 | async-start | bytes 393216 | tf_op jit(solution)/shard_map/all_to_all | solution.py:125
  331.0 1.1 copy-start.20
  331.0 1.1 copy-start.22
  352.5 17.4 %all-to-all-start.1 = ((bf16[16,2,3072]{2,1,0:T(2,128)(2,1)}), bf16[16,2,3072]{2,1,0:T(2,128)(2,1)S(1)}, u32[]{:S(2)}, u32[]{:S(2)}) async-start(bf16[16,2,3072]{2,1,0:T(2,128)(2,1)} %reshape.284), calls=%async_computation.1 | async-start | bytes 393216 | tf_op jit(solution)/shard_map/all_to_all | solution.py:99
  369.9 13.0 %all-to-all-start.2 = ((bf16[16,2,3072]{2,1,0:T(2,128)(2,1)}), bf16[16,2,3072]{2,1,0:T(2,128)(2,1)S(1)}, u32[]{:S(2)}, u32[]{:S(2)}) async-start(bf16[16,2,3072]{2,1,0:T(2,128)(2,1)} %reshape.282), calls=%async_computation.2 | async-start | bytes 393216 | tf_op jit(solution)/shard_map/all_to_all | solution.py:100
  383.1 4.0 copy-start.4
  383.1 4.0 copy-start.5
  383.1 4.0 copy-start.12
  390.5 2.3 copy-start.31
  390.5 2.3 copy-start.33
  476.7 87.1 %all-to-all-start.3 = ((bf16[16,2,3072]{2,1,0:T(2,128)(2,1)}), bf16[16,2,3072]{2,1,0:T(2,128)(2,1)}, u32[]{:S(2)}, u32[]{:S(2)}) async-start(bf16[16,2,3072]{2,1,0:T(2,128)(2,1)} %reshape.286), calls=%async_computation.3 | async-start | bytes 393216 | tf_op jit(solution)/shard_map/all_to_all | solution.py:124
  563.9 31.4 %all-to-all-start.4 = ((bf16[16,2,3072]{2,1,0:T(2,128)(2,1)}), bf16[16,2,3072]{2,1,0:T(2,128)(2,1)S(1)}, u32[]{:S(2)}, u32[]{:S(2)}) async-start(bf16[16,2,3072]{2,1,0:T(2,128)(2,1)} %reshape.288), calls=%async_computation.4 | async-start | bytes 393216 | tf_op jit(solution)/shard_map/all_to_all | solution.py:125
  635.0 1.1 copy-start.6
  635.0 1.1 copy-start.13
  635.6 9.3 %copy-start.7 = (f32[8,16,768]{2,1,0:T(8,128)S(1)}, f32[8,16,768]{2,1,0:T(8,128)}, u32[]{:S(2)}) copy-start(f32[8,16,768]{2,1,0:T(8,128)} %get-tuple-element.55) | copy-start | bytes 1179652
  636.9 4.8 collective-permute-start.2
  641.7 10.3 %collective-permute-start.3 = (bf16[1,2,2304]{2,1,0:T(2,128)(2,1)S(1)}, bf16[1,2,2304]{2,1,0:T(2,128)(2,1)S(1)}, u32[]{:S(2)}, u32[]{:S(2)}) collective-permute-start(bf16[1,2,2304]{2,1,0:T(2,128)(2,1)S(1)} %slice.145), channel_id=1, source_target_pairs={{16,0},{32,16},{48,32},{64,48},{80,64},{96,80},{112,96},{128,112},... | collective-permute-start | bytes 27656 | tf_op jit(solution)/shard_map/ppermute | solution.py:17
  651.9 1.3 copy-start
  651.9 1.6 copy-start.1
  657.8 2.0 copy-start.2
  741.5 2.2 copy-start.8
  741.5 2.2 copy-start.9
  741.5 2.3 copy-start.15
  741.5 2.3 copy-start.17
  741.5 2.3 copy-start.19
  741.5 2.3 copy-start.21
  741.5 2.3 copy-start.23
  741.5 2.3 copy-start.25
  741.5 2.3 copy-start.27
  741.5 2.3 copy-start.29
where the time goes:
time: 756 us; the launch traced here: 745 us
  other arithmetic  288 us (38%)
  local copies, waits for them, and re-layouts  200 us (26%)
  blocking collectives  117 us (15%)
  starting transfers between devices  67.5 us (9%)
  waiting for transfers between devices  41.5 us (5%)
  matrix products  28.6 us (4%)
    unnamed x8, other arithmetic  278 us
    unnamed x101, local copies, waits for them, and re-layouts  77 us
    psum x1, blocking collectives, per_device(): weight_grad = lax.psum(local_terms, ('row', 'col')) / math.sqrt(seq_total)  75.8 us
    all_to_all x2, blocking collectives, restore(): lax.all_to_all(scaled, 'row', split_axis=1, concat_axis=3, tiled=True)  30.3 us
    all_to_all x2, local copies, waits for them, and re-layouts, restore(): lax.all_to_all(turned_re, 'col', split_axis=2, concat_axis=1, tiled=True)  22.6 us
    all_to_all x2, local copies, waits for them, and re-layouts, restore(): lax.all_to_all(turned_im, 'col', split_axis=2, concat_axis=1, tiled=True)  22.6 us
    reshape x4, local copies, waits for them, and re-layouts, restore(): turned_re = (inner_re * inv_cos - inner_im * inv_sin).astype(jnp.bfloat16...  21.8 us
    reshape x4, local copies, waits for them, and re-layouts, restore(): turned_im = (inner_im * inv_cos + inner_re * inv_sin).astype(jnp.bfloat16...  21.2 us
  transfers between devices with their start and end apart: 13, of which 8 were waited for; matrix products, arithmetic and copies ran while one was open for 31% of the time, Pallas kernels for 0%

commit v1 on v0

v1 whole, which is shorter than its diff:
```python
import functools
import math

import jax
import jax.numpy as jnp
import ml_dtypes
import numpy as np
from jax import lax
from jax.experimental import pallas as pl
from jax.experimental.pallas import tpu as pltpu
from jax.sharding import PartitionSpec as P

MESH = pl.DeviceIdType.MESH
F32 = jnp.float32
BF16 = jnp.bfloat16

NP = 16
DL = 48
GR = 16
N1 = 128
N2 = 256
SEQ = N1 * N2

XR, CR, FM, HX, SS, GG, YY, ZZ, GM, HG, D1, MR, IR, D2 = range(14)


def slot_freq(col, slot):
    return 8 * col + slot + (1 if col >= 8 else 0)


def tables():
    lane_n1 = np.array([8 * (l % 16) + l // 16 for l in range(128)])
    first = np.zeros((128, 128))
    last = np.zeros((128, 128))
    for col in range(16):
        for slot in range(4):
            k1 = slot_freq(col, slot)
            turn = 2 * np.pi * (lane_n1 * k1 % 128) / 128
            re_row, im_row = slot * 16 + col, (slot + 4) * 16 + col
            if k1 == 0:
                first[:, re_row] = 1.0
                first[:, im_row] = np.cos(np.pi * lane_n1)
                last[re_row] = 1.0
                last[im_row] = np.cos(np.pi * lane_n1)
            else:
                first[:, re_row] = np.cos(turn)
                first[:, im_row] = -np.sin(turn)
                last[re_row] = np.cos(turn)
                last[im_row] = -np.sin(turn)
    last = last / SEQ
    idx = np.arange(N2)
    angle = 2 * np.pi * (idx[:, None] * idx[None, :] % N2) / N2
    second = np.concatenate([np.cos(angle), np.sin(angle)], 1)
    fwd = np.zeros((16, 2, 16, 128), np.float32)
    inv = np.zeros((16, 2, 8, N2), np.float32)
    low = np.arange(16)
    for col in range(16):
        for target in range(16):
            for slot in range(4):
                k1 = slot_freq(target, slot)
                turn = 2 * np.pi * (k1 * (16 * col + low) % SEQ) / SEQ
                re_l, im_l = slot * 16 + low, (slot + 4) * 16 + low
                fwd[col, 0, target, re_l] = np.cos(turn)
                fwd[col, 0, target, im_l] = np.cos(turn)
                fwd[col, 1, target, re_l] = np.sin(turn)
                fwd[col, 1, target, im_l] = -np.sin(turn)
        for slot in range(5):
            k1 = slot_freq(col, slot) if slot < 4 else 64
            turn = 2 * np.pi * (k1 * idx % SEQ) / SEQ
            inv[col, 0, slot] = np.cos(turn)
            inv[col, 1, slot] = np.sin(turn)
    return (
        first.astype(ml_dtypes.bfloat16),
        last.astype(ml_dtypes.bfloat16),
        second.astype(ml_dtypes.bfloat16),
        fwd,
        inv,
    )


def swap_bits(planes, pairs):
    lane = lax.broadcasted_iota(jnp.int32, planes[0].shape, 1)
    planes = list(planes)
    for plane_bit, lane_bit in pairs:
        shift = 1 << lane_bit
        upper = (lane & shift) != 0
        for i in range(len(planes)):
            if i & (1 << plane_bit):
                continue
            j = i | (1 << plane_bit)
            low, high = planes[i], planes[j]
            planes[i] = jnp.where(upper, pltpu.roll(high, shift, 1), low)
            planes[j] = jnp.where(upper, high, pltpu.roll(low, 128 - shift, 1))
    return planes


LOW4 = ((0, 0), (1, 1), (2, 2), (3, 3))
HIGH3 = ((0, 4), (1, 5), (2, 6))


def kernel(
    x_ref, w_ref, cot_ref, fr_ref, fi_ref, first_ref, last_ref, second_ref, fwd_ref, inv_ref,
    mixed_ref, ig_ref, fgr_ref, fgi_ref, dw_ref,
    xt, xrecv, ct, crecv, w9, wt, wb, fo, fm, rev, fh, tf, ti,
    xp, hx_send, hx_recv, cp, ap, bp, sp, yp, fld,
    s_send, s_recv, g_send, g_recv, y_send, y_recv, z_send, z_recv,
    pp, uu, sr, si, qq, gs_send, gm_recv, gp, hg_send, hg_recv,
    d1_send, d1_recv, d2_send, d2_recv, m_send, m_recv, i_send, i_recv,
    send_sem, recv_sem, local_sem,
):
    row = lax.axis_index("row")
    col = lax.axis_index("col")
    low_half = col < 8

    def remote(src, dst, which, target):
        return pltpu.make_async_remote_copy(
            src_ref=src,
            dst_ref=dst,
            send_sem=send_sem.at[which],
            recv_sem=recv_sem.at[which],
            device_id=target,
            device_id_type=MESH,
        )

    def exchange(axis, me, which, src_at, dst):
        def body(step, carry):
            peer = lax.rem(me + step, NP)
            remote(src_at(peer), dst, which, {axis: peer}).start()
            return carry

        lax.fori_loop(1, NP, body, 0)

    def wait_bytes(ref, sem):
        pltpu.make_async_copy(ref, ref, sem).wait()

    def tile_of(ref, peer):
        return ref.at[pl.ds(pl.multiple_of(peer * DL, DL), DL)]

    def over_groups(body):
        def step(g, carry):
            body(pl.ds(pl.multiple_of(g * GR, GR), GR))
            return carry

        lax.fori_loop(0, DL // GR, step, 0)

    loads = [
        pltpu.make_async_copy(fr_ref, fo.at[0], local_sem.at[0]),
        pltpu.make_async_copy(fi_ref, fo.at[1], local_sem.at[1]),
        pltpu.make_async_copy(fwd_ref.at[col], tf, local_sem.at[2]),
        pltpu.make_async_copy(inv_ref.at[col], ti, local_sem.at[3]),
    ]
    for load in loads:
        load.start()

    barrier = pltpu.get_barrier_semaphore()

    def greet(step, carry):
        pl.semaphore_signal(
            barrier, inc=1, device_id={"row": lax.rem(row + step, NP)}, device_id_type=MESH
        )
        pl.semaphore_signal(
            barrier, inc=1, device_id={"col": lax.rem(col + step, NP)}, device_id_type=MESH
        )
        return carry

    lax.fori_loop(1, NP, greet, 0)

    def turn_home(src_ref, dst):
        for i in range(6):
            block = src_ref[:, :, 128 * i : 128 * (i + 1)].reshape(128, 128).astype(F32)
            dst[128 * i : 128 * (i + 1), :] = block.T.astype(BF16)

    turn_home(x_ref, xt)
    pl.semaphore_wait(barrier, 2 * (NP - 1))

    exchange("row", row, XR, lambda p: tile_of(xt, p), tile_of(xrecv, row))
    own_rows = pl.ds(pl.multiple_of(row * DL, DL), DL)
    xrecv[own_rows, :] = xt[own_rows, :]
    turn_home(cot_ref, ct)
    exchange("row", row, CR, lambda p: tile_of(ct, p), tile_of(crecv, row))
    crecv[own_rows, :] = ct[own_rows, :]

    partner = 15 - col
    extra_row = jnp.where(low_half, 4, 0)
    extra_to = jnp.where(low_half, partner, lax.rem(16 - col, 8))
    for part, ref in enumerate((fr_ref, fi_ref)):
        remote(ref.at[pl.ds(5, 3)], fm.at[part, pl.ds(1, 3)], FM, {"col": partner}).start()
        remote(ref.at[extra_row], fm.at[part, 0], FM, {"col": extra_to}).start()

    w9[...] = jnp.zeros_like(w9)
    for tap in range(3):
        for stream in range(3):
            q = 3 * tap + stream
            w9[q : q + 1, :] = w_ref[tap : tap + 1, 768 * stream : 768 * (stream + 1)]
    for i in range(6):
        wt[128 * i : 128 * (i + 1), :] = w9[:, 128 * i : 128 * (i + 1)].T
    columns = wt[own_rows, :]
    for q in range(9):
        wb[q] = jnp.broadcast_to(columns[:, q : q + 1], (DL, 128))
    for load in loads:
        load.wait()

    lane = lax.broadcasted_iota(jnp.int32, (DL, 128), 1)

    def planes_in(recv, dst, base):
        def body(rows):
            planes = [recv[i, rows, :].astype(F32) for i in range(NP)]
            planes = swap_bits(planes, LOW4)
            for i in range(NP):
                dst[base + i, rows, :] = planes[i]

        over_groups(body)

    def tiles_out(src, dst, table):
        def body(rows):
            flat = src[:, rows, :].reshape(NP * GR, 128)
            out = jnp.dot(flat, first_ref[...], preferred_element_type=F32).reshape(NP, GR, 128)
            tiles = swap_bits([out[i] for i in range(NP)], LOW4)
            for i in range(NP):
                turned = tiles[i] * tf[0, i : i + 1, :] + pltpu.roll(tiles[i], 64, 1) * tf[1, i : i + 1, :]
                dst[i, rows, :] = turned.astype(BF16)

        over_groups(body)

    wait_bytes(xrecv.at[pl.ds(0, 15 * DL)], recv_sem.at[XR])
    x3 = xrecv.reshape(NP, DL, 128)
    planes_in(x3, xp, 2)
    hx_send[0] = xp[16].astype(BF16)
    hx_send[1] = xp[17].astype(BF16)
    remote(hx_send, hx_recv, HX, {"col": lax.rem(col + 1, NP)}).start()

    wait_bytes(hx_recv, recv_sem.at[HX])
    for i in range(2):
        halo = hx_recv[i].astype(F32)
        back = jnp.where(lane >= 16, pltpu.roll(halo, 16, 1), pltpu.roll(halo, 17, 1))
        back = jnp.where(lane == 0, 0.0, back)
        xp[i] = jnp.where(col == 0, back, halo)

    def streams(rows):
        taps = [wb[q, rows, :] for q in range(9)]
        behind2, behind1 = xp[0, rows, :], xp[1, rows, :]
        for i in range(NP):
            now = xp[i + 2, rows, :]
            z = [taps[j] * now + taps[3 + j] * behind1 + taps[6 + j] * behind2 for j in range(3)]
            ap[i, rows, :] = z[0]
            bp[i, rows, :] = z[1]
            sp[i, rows, :] = z[2]
            fld[i, rows, :] = (z[0] * z[1]).astype(BF16)
            behind2, behind1 = behind1, now

    over_groups(streams)
    tiles_out(fld, s_send, tf)
    exchange("col", col, SS, lambda p: s_send.at[p], s_recv.at[col])
    s_recv[col] = s_send[col]

    wait_bytes(crecv.at[pl.ds(0, 15 * DL)], recv_sem.at[CR])
    planes_in(crecv.reshape(NP, DL, 128), cp, 0)

    def gate_grad(rows):
        for i in range(NP):
            fld[i, rows, :] = (cp[i, rows, :] * sp[i, rows, :]).astype(BF16)

    over_groups(gate_grad)
    tiles_out(fld, g_send, tf)
    exchange("col", col, GG, lambda p: g_send.at[p], g_recv.at[col])
    g_recv[col] = g_send[col]

    wait_bytes(fm, recv_sem.at[FM])
    at_row = lax.broadcasted_iota(jnp.int32, (N2, N2), 0)
    at_col = lax.broadcasted_iota(jnp.int32, (N2, N2), 1)
    reverse = jnp.where(at_row + at_col == N2 - 1, 1.0, 0.0).astype(BF16)
    rev[...] = jnp.dot(
        fm[...].reshape(8 * DL, N2), reverse, preferred_element_type=F32
    ).reshape(2, 4, DL, N2)

    def mirror_at(slot):
        return jnp.where(low_half, (4 - slot) % 4, 3 - slot)

    own_at = jnp.where(low_half, 0, 1)
    for slot in range(4):
        rev_re = rev[0, mirror_at(slot)]
        rev_im = -rev[1, mirror_at(slot)]
        if slot == 0:
            fh[0, 4] = rev_re
            fh[1, 4] = rev_im
            rev_re = jnp.where(col == 0, 0.0, rev_re)
            rev_im = jnp.where(col == 0, 0.0, rev_im)
        fh[0, slot] = fo[0, own_at + slot].astype(F32) + rev_re
        fh[1, slot] = fo[1, own_at + slot].astype(F32) + rev_im

    parts = [(0, 4), (1, 5), (2, 6), (3, 7), (8, 9)]

    def spectrum(recv):
        def body(rows):
            planes = swap_bits([recv[i, rows, :].astype(F32) for i in range(NP)], HIGH3)
            for i in range(NP):
                half = i // 8
                pp[i % 8, rows, 128 * half : 128 * (half + 1)] = planes[i].astype(BF16)

        over_groups(body)
        middle = pp[4].astype(F32)
        pp[8] = (middle * ti[0, 4:5, :]).astype(BF16)
        pp[9] = (-middle * ti[1, 4:5, :]).astype(BF16)
        pp[4] = jnp.where(col == 0, 0.0, middle).astype(BF16)
        uu[...] = jnp.dot(
            pp[...].reshape(10 * DL, N2), second_ref[...], preferred_element_type=F32
        ).reshape(10, DL, 2 * N2)

    def value(slot):
        re, im = parts[slot]
        return (
            uu[re, :, :N2] + uu[im, :, N2:],
            uu[im, :, :N2] - uu[re, :, N2:],
        )

    def restore(dst):
        uu[...] = jnp.dot(
            pp[...].reshape(10 * DL, N2), second_ref[...], preferred_element_type=F32
        ).reshape(10, DL, 2 * N2)
        for slot in range(4):
            re, im = parts[slot]
            z_re = uu[re, :, :N2] - uu[im, :, N2:]
            z_im = uu[im, :, :N2] + uu[re, :, N2:]
            cos, sin = ti[0, slot : slot + 1, :], ti[1, slot : slot + 1, :]
            qq[slot] = z_re * cos - z_im * sin
            q_im = z_im * cos + z_re * sin
            if slot == 0:
                re4, im4 = parts[4]
                z_re4 = uu[re4, :, :N2] - uu[im4, :, N2:]
                z_im4 = uu[im4, :, :N2] + uu[re4, :, N2:]
                q_im = jnp.where(col == 0, z_re4 * ti[0, 4:5, :] - z_im4 * ti[1, 4:5, :], q_im)
            qq[4 + slot] = q_im

        def body(rows):
            planes = [
                qq[i % 8, rows, 128 * (i // 8) : 128 * (i // 8 + 1)] for i in range(NP)
            ]
            planes = swap_bits(planes, HIGH3)
            for i in range(NP):
                dst[i, rows, :] = planes[i].astype(BF16)

        over_groups(body)

    wait_bytes(s_recv.at[pl.ds(0, 15)], recv_sem.at[SS])
    spectrum(s_recv)
    for slot in range(5):
        re, im = parts[slot]
        s_re, s_im = value(slot)
        sr[slot] = s_re
        si[slot] = s_im
        f_re, f_im = fh[0, slot], fh[1, slot]
        pp[re] = (s_re * f_re - s_im * f_im).astype(BF16)
        pp[im] = (s_re * f_im + s_im * f_re).astype(BF16)
    restore(y_send)
    exchange("col", col, YY, lambda p: y_send.at[p], y_recv.at[col])
    y_recv[col] = y_send[col]

    wait_bytes(g_recv.at[pl.ds(0, 15)], recv_sem.at[GG])
    spectrum(g_recv)
    for slot in range(5):
        re, im = parts[slot]
        g_re, g_im = value(slot)
        f_re, f_im = fh[0, slot], fh[1, slot]
        pp[re] = (g_re * f_re + g_im * f_im).astype(BF16)
        pp[im] = (g_im * f_re - g_re * f_im).astype(BF16)
        s_re, s_im = sr[slot], si[slot]
        grad_re = (s_re * g_re + s_im * g_im) * (1.0 / SEQ)
        grad_im = (s_re * g_im - s_im * g_re) * (1.0 / SEQ)
        if slot < 4:
            fgr_ref[own_at + slot] = grad_re
            fgi_ref[own_at + slot] = grad_im
            gs_send[0, mirror_at(slot)] = grad_re.astype(BF16)
            gs_send[1, mirror_at(slot)] = grad_im.astype(BF16)
        else:
            gs_send[0, 0] = jnp.where(col == 0, grad_re, gs_send[0, 0].astype(F32)).astype(BF16)
            gs_send[1, 0] = jnp.where(col == 0, grad_im, gs_send[1, 0].astype(F32)).astype(BF16)
    restore(z_send)
    exchange("col", col, ZZ, lambda p: z_send.at[p], z_recv.at[col])
    z_recv[col] = z_send[col]
    back_to = jnp.where(low_half, jnp.where(col == 0, 8, 16 - col), partner)
    back_to = lax.rem(back_to, NP)
    for part in range(2):
        remote(gs_send.at[part, pl.ds(1, 3)], gm_recv.at[part, pl.ds(1, 3)], GM, {"col": partner}).start()
        remote(gs_send.at[part, 0], gm_recv.at[part, 0], GM, {"col": back_to}).start()

    def field_back(recv, dst):
        def body(rows):
            planes = swap_bits([recv[i, rows, :].astype(F32) for i in range(NP)], LOW4)
            flat = jnp.stack([p.astype(BF16) for p in planes]).reshape(NP * GR, 128)
            out = jnp.dot(flat, last_ref[...], preferred_element_type=F32)
            dst[:, rows, :] = out.astype(BF16).astype(F32).reshape(NP, GR, 128)

        over_groups(body)

    def send_home(make, dst):
        def body(rows):
            tiles = swap_bits([make(i, rows) for i in range(NP)], LOW4)
            for i in range(NP):
                dst[i, rows, :] = tiles[i].astype(BF16)

        over_groups(body)

    wait_bytes(y_recv.at[pl.ds(0, 15)], recv_sem.at[YY])
    field_back(y_recv, yp)
    send_home(lambda i, rows: sp[i, rows, :] * yp[i, rows, :], m_send)
    exchange("row", row, MR, lambda p: m_send.at[p], tile_of(m_recv, row))
    m_recv[own_rows, :] = m_send[row]

    wait_bytes(z_recv.at[pl.ds(0, 15)], recv_sem.at[ZZ])
    field_back(z_recv, gp)

    def rounded(value):
        return value.astype(BF16).astype(F32)

    def stream_grads(rows):
        taps = [wb[q, rows, :] for q in range(9)]
        sums = [jnp.zeros((GR, 128), F32)] * 9
        before1 = before2 = None
        for i in range(NP):
            gs = gp[i, rows, :]
            grads = (
                rounded(gs * bp[i, rows, :]),
                rounded(gs * ap[i, rows, :]),
                rounded(cp[i, rows, :] * yp[i, rows, :]),
            )
            at_tap = [
                taps[3 * t] * grads[0] + taps[3 * t + 1] * grads[1] + taps[3 * t + 2] * grads[2]
                for t in range(3)
            ]
            past = [xp[i + 2 - t, rows, :] for t in range(3)]
            sums = [sums[q] + past[q // 3] * grads[q % 3] for q in range(9)]
            if i == 0:
                hg_send[0, rows, :] = at_tap[2].astype(BF16)
                first_one = at_tap[1]
            if i == 1:
                hg_send[1, rows, :] = (first_one + at_tap[2]).astype(BF16)
            if before2 is not None:
                gp[i - 2, rows, :] = before2 + at_tap[2]
            before2 = None if before1 is None else before1 + at_tap[1]
            before1 = at_tap[0]
        gp[14, rows, :] = before2
        gp[15, rows, :] = before1
        at = lax.broadcasted_iota(jnp.int32, (GR, 128), 1)
        total = jnp.zeros((GR, 128), F32)
        for q in range(9):
            total = jnp.where(at == q, jnp.sum(sums[q], axis=1, keepdims=True), total)
        wt[rows, :] = total[:, :16]

    over_groups(stream_grads)
    remote(hg_send, hg_recv, HG, {"col": lax.rem(col + NP - 1, NP)}).start()
    d1_send[...] = jnp.zeros_like(d1_send)
    d1_send[:, :DL] = wt[:DL, :].T * (1.0 / math.sqrt(SEQ))
    exchange("col", col, D1, lambda p: d1_send, d1_recv.at[col])
    d1_recv[col] = d1_send[...]

    wait_bytes(hg_recv, recv_sem.at[HG])
    for i in range(2):
        halo = hg_recv[i].astype(F32)
        ahead = jnp.where(lane < 112, pltpu.roll(halo, 112, 1), pltpu.roll(halo, 111, 1))
        ahead = jnp.where(lane == 127, 0.0, ahead)
        gp[14 + i] = gp[14 + i] + jnp.where(col == NP - 1, ahead, halo)
    send_home(lambda i, rows: gp[i, rows, :], i_send)
    exchange("row", row, IR, lambda p: i_send.at[p], tile_of(i_recv, row))
    i_recv[own_rows, :] = i_send[row]

    wait_bytes(gm_recv, recv_sem.at[GM])
    rev[...] = jnp.dot(
        gm_recv[...].reshape(8 * DL, N2), reverse, preferred_element_type=F32
    ).reshape(2, 4, DL, N2)
    fgr_ref[extra_row] = rev[0, 0]
    fgi_ref[extra_row] = -rev[1, 0]
    for i in range(1, 4):
        fgr_ref[4 + i] = rev[0, i]
        fgi_ref[4 + i] = -rev[1, i]

    wait_bytes(d1_recv.at[pl.ds(0, 15)], recv_sem.at[D1])
    total = d1_recv[0]
    for i in range(1, NP):
        total = total + d1_recv[i]
    d2_send[...] = total
    exchange("row", row, D2, lambda p: d2_send, d2_recv.at[row])
    d2_recv[row] = total

    def home(src, dst_ref):
        for i in range(6):
            block = src[128 * i : 128 * (i + 1), :].astype(F32).T
            dst_ref[:, :, 128 * i : 128 * (i + 1)] = block.astype(BF16).reshape(8, 16, 128)

    wait_bytes(m_recv.at[pl.ds(0, 15 * DL)], recv_sem.at[MR])
    home(m_recv, mixed_ref)
    wait_bytes(d2_recv.at[pl.ds(0, 15)], recv_sem.at[D2])
    spot = lax.broadcasted_iota(jnp.int32, (16, 128), 1)
    blocks = [jnp.zeros((16, 128), F32)] * 6
    for i in range(NP):
        block, off = divmod(DL * i, 128)
        piece = pltpu.roll(d2_recv[i], off, 1) if off else d2_recv[i]
        if off + DL > 128:
            blocks[block] = blocks[block] + jnp.where(spot >= off, piece, 0.0)
            blocks[block + 1] = blocks[block + 1] + jnp.where(spot < off, piece, 0.0)
        else:
            blocks[block] = blocks[block] + piece
    for tap in range(3):
        for stream in range(3):
            q = 3 * tap + stream
            for i in range(6):
                at = 768 * stream + 128 * i
                dw_ref[tap : tap + 1, at : at + 128] = blocks[i][q : q + 1, :]
    wait_bytes(i_recv.at[pl.ds(0, 15 * DL)], recv_sem.at[IR])
    home(i_recv, ig_ref)

    wait_bytes(xt.at[pl.ds(0, 15 * DL)], send_sem.at[XR])
    wait_bytes(ct.at[pl.ds(0, 15 * DL)], send_sem.at[CR])
    wait_bytes(fm, send_sem.at[FM])
    wait_bytes(hx_send, send_sem.at[HX])
    for ref, which in (
        (s_send, SS), (g_send, GG), (y_send, YY), (z_send, ZZ), (m_send, MR), (i_send, IR),
        (d1_recv, D1), (d2_recv, D2),
    ):
        wait_bytes(ref.at[pl.ds(0, 15)], send_sem.at[which])
    wait_bytes(gs_send, send_sem.at[GM])
    wait_bytes(hg_send, send_sem.at[HG])


def per_device(sequence, conv_weights, cotangent, filter_re, filter_im):
    first, last, second, fwd, inv = (jnp.asarray(t) for t in tables())
    vmem = pl.BlockSpec(memory_space=pltpu.VMEM)
    hbm = pl.BlockSpec(memory_space=pl.ANY)
    tiles = pltpu.VMEM((NP, DL, 128), BF16)
    planes = pltpu.VMEM((NP, DL, 128), F32)
    flat = pltpu.VMEM((NP * DL, 128), BF16)
    spec = pltpu.VMEM((2, 4, DL, N2), BF16)
    pair = pltpu.VMEM((2, DL, 128), BF16)
    small = pltpu.VMEM((NP, 16, 128), F32)
    one = pltpu.VMEM((16, 128), F32)
    return pl.pallas_call(
        kernel,
        out_shape=(
            jax.ShapeDtypeStruct(sequence.shape, BF16),
            jax.ShapeDtypeStruct(sequence.shape, BF16),
            jax.ShapeDtypeStruct(filter_re.shape, F32),
            jax.ShapeDtypeStruct(filter_re.shape, F32),
            jax.ShapeDtypeStruct(conv_weights.shape, F32),
        ),
        in_specs=[vmem, vmem, vmem, hbm, hbm, vmem, vmem, vmem, hbm, hbm],
        out_specs=[vmem] * 5,
        scratch_shapes=[
            flat, flat, flat, flat,
            pltpu.VMEM((16, 768), F32),
            pltpu.VMEM((768, 16), F32),
            pltpu.VMEM((9, DL, 128), F32),
            pltpu.VMEM((2, 8, DL, N2), BF16),
            spec,
            pltpu.VMEM((2, 4, DL, N2), F32),
            pltpu.VMEM((2, 5, DL, N2), F32),
            pltpu.VMEM((2, 16, 128), F32),
            pltpu.VMEM((2, 8, N2), F32),
            pltpu.VMEM((NP + 2, DL, 128), F32),
            pair, pair,
            planes, planes, planes, planes, planes,
            tiles,
            tiles, tiles, tiles, tiles, tiles, tiles, tiles, tiles,
            pltpu.VMEM((10, DL, N2), BF16),
            pltpu.VMEM((10, DL, 2 * N2), F32),
            pltpu.VMEM((5, DL, N2), F32),
            pltpu.VMEM((5, DL, N2), F32),
            pltpu.VMEM((8, DL, N2), F32),
            spec, spec,
            planes,
            pair, pair,
            one, small, one, small,
            tiles, flat, tiles, flat,
            pltpu.SemaphoreType.DMA((14,)),
            pltpu.SemaphoreType.DMA((14,)),
            pltpu.SemaphoreType.DMA((4,)),
        ],
        compiler_params=pltpu.CompilerParams(
            collective_id=0, has_side_effects=True, vmem_limit_bytes=40 * 1024 * 1024
        ),
    )(
        sequence, conv_weights, cotangent, filter_re, filter_im,
        first, last, second, fwd, inv,
    )


def solution(mesh):
    return jax.shard_map(
        per_device,
        mesh=mesh,
        in_specs=(
            P("row", "col", None),
            P(),
            P("row", "col", None),
            P("col", "row", None),
            P("col", "row", None),
        ),
        out_specs=(
            P("row", "col", None),
            P("row", "col", None),
            P("col", "row", None),
            P("col", "row", None),
            P(),
        ),
        check_vma=False,
    )
```

time: 756 us -> 78.4 us (0.10); the launches traced: 745 us -> 77.9 us
  other arithmetic: 288 us -> 0 us
  local copies, waits for them, and re-layouts: 200 us -> 12.3 us
  blocking collectives: 117 us -> 0 us
  starting transfers between devices: 67.5 us -> 0 us
  Pallas kernels: 0 us -> 65 us
  waiting for transfers between devices: 41.5 us -> 0 us
  matrix products: 28.6 us -> 0 us
    unnamed x8 -> x0, other arithmetic: 278 us -> none
    psum x1 -> x0, blocking collectives: 75.8 us -> none  [per_device(): weight_grad = lax.psum(local_terms, ('row', 'col')) / math.sqrt(seq_total)]
    pallas_call x0 -> x1, Pallas kernels: none -> 65 us  [per_device(): pl.pallas_call(kernel, out_shape=(jax.ShapeDtypeStruct(sequence.shape, BF...]
    unnamed x101 -> x25, local copies, waits for them, and re-layouts: 77 us -> 12.3 us
    all_to_all x9 -> x0, starting transfers between devices: 52.8 us -> none  [the longest x2 15.4 us: restore(): lax.all_to_all(turned_im, 'col', split_axis=2, concat_axis=1, tiled=True)]
    reshape x14 -> x0, local copies, waits for them, and re-layouts: 48.9 us -> none  [the longest x4 21.8 us: restore(): turned_re = (inner_re * inv_cos - inner_im * inv_sin).astype(jnp.bfloat16...]
    all_to_all x10 -> x0, local copies, waits for them, and re-layouts: 47.2 us -> none  [the longest x2 22.6 us: restore(): lax.all_to_all(turned_re, 'col', split_axis=2, concat_axis=1, tiled=True)]
    all_to_all x3 -> x0, blocking collectives: 41.5 us -> none  [the longest x2 30.3 us: restore(): lax.all_to_all(scaled, 'row', split_axis=1, concat_axis=3, tiled=True)]
  transfers between devices with their start and end apart: 13 -> 0, of which waited for: 8 -> 0; matrix products, arithmetic and copies ran while one was open for 31% -> 0% of each run, Pallas kernels for 0% -> 0%
where the time goes in v1:
time: 78.4 us; the launch traced here: 77.9 us
  Pallas kernels  65 us (83%)
  local copies, waits for them, and re-layouts  12.3 us (16%)
    pallas_call x1, Pallas kernels, per_device(): pl.pallas_call(kernel, out_shape=(jax.ShapeDtypeStruct(sequence.shape, BF...  65 us
    unnamed x25, local copies, waits for them, and re-layouts  12.3 us

profile of v1, /device:TPU:1, one launch (start us, length us, event | category | flops | bytes accessed | tf_op | source)
XLA Modules:
  0.0 77.9 jit_solution(4673772506530670867)
XLA Ops:
  0.6 0.0 copy-start
  0.6 0.9 %copy-done = f32[16,2,8,256]{3,2,1,0:T(8,128)S(1)} copy-done((f32[16,2,8,256]{3,2,1,0:T(8,128)S(1)}, f32[16,2,8,256]{3,2,1,0:T(8,128)}, u32[]{:S(2)}) %copy-start) | copy-done | bytes 262168
  1.6 0.0 copy-start.1
  1.6 0.9 %copy-done.1 = f32[16,2,16,128]{3,2,1,0:T(8,128)S(1)} copy-done((f32[16,2,16,128]{3,2,1,0:T(8,128)S(1)}, f32[16,2,16,128]{3,2,1,0:T(8,128)}, u32[]{:S(2)}) %copy-start.1) | copy-done | bytes 262168
  2.5 0.0 copy-start.2
  2.5 0.9 %copy-done.2 = bf16[256,512]{1,0:T(8,128)(2,1)S(1)} copy-done((bf16[256,512]{1,0:T(8,128)(2,1)S(1)}, bf16[256,512]{1,0:T(8,128)(2,1)}, u32[]{:S(2)}) %copy-start.2) | copy-done | bytes 262168
  3.5 0.0 copy-start.3
  3.5 0.9 %copy-done.3 = bf16[8,16,768]{2,1,0:T(8,128)(2,1)S(1)} copy-done((bf16[8,16,768]{2,1,0:T(8,128)(2,1)S(1)}, bf16[8,16,768]{2,1,0:T(8,128)(2,1)}, u32[]{:S(2)}) %copy-start.3) | copy-done | bytes 196632
  4.4 0.0 copy-start.4
  4.4 0.9 %copy-done.4 = bf16[8,16,768]{2,1,0:T(8,128)(2,1)S(1)} copy-done((bf16[8,16,768]{2,1,0:T(8,128)(2,1)S(1)}, bf16[8,16,768]{2,1,0:T(8,128)(2,1)}, u32[]{:S(2)}) %copy-start.4) | copy-done | bytes 196632
  5.3 0.0 copy-start.5
  5.3 0.9 %copy-done.5 = bf16[8,48,256]{2,1,0:T(8,128)(2,1)S(1)} copy-done((bf16[8,48,256]{2,1,0:T(8,128)(2,1)S(1)}, bf16[8,48,256]{2,1,0:T(8,128)(2,1)}, u32[]{:S(2)}) %copy-start.5) | copy-done | bytes 196632
  6.3 0.0 copy-start.6
  6.3 0.9 %copy-done.6 = bf16[8,48,256]{2,1,0:T(8,128)(2,1)S(1)} copy-done((bf16[8,48,256]{2,1,0:T(8,128)(2,1)S(1)}, bf16[8,48,256]{2,1,0:T(8,128)(2,1)}, u32[]{:S(2)}) %copy-start.6) | copy-done | bytes 196632
  7.2 0.0 copy-start.7
  7.2 0.8 copy-done.7
  8.0 0.0 copy-start.8
  8.0 0.8 copy-done.8
  8.7 0.0 copy-start.9
  8.7 0.8 copy-done.9
  9.5 65.0 %shard_map.137 = (bf16[8,16,768]{2,1,0:T(8,128)(2,1)S(1)}, bf16[8,16,768]{2,1,0:T(8,128)(2,1)S(1)}, f32[8,48,256]{2,1,0:T(8,128)S(1)}, f32[8,48,256]{2,1,0:T(8,128)S(1)}, f32[3,2304]{1,0:T(4,128)S(1)}) custom-call(bf16[8,16,768]{2,1,0:T(8,128)(2,1)S(1)} %copy-done.3, f32[3,2304]{1,0:T(4,128)S(1)} %copy-done.7, bf16[8,16,768]{2,1,0:T(8,128)(2,1)S(1)} %copy-done.4, ...), custom_call_target="tpu_custom_call" | custom-call | tf_op jit(solution)/shard_map/pallas_call | solution.py:535
  74.4 0.7 copy.20
  75.1 0.7 copy.21
  75.8 0.7 copy.22
  76.5 0.7 copy.23
  77.3 0.6 copy.24
Async XLA Ops:
  0.6 1.0 %copy-start = (f32[16,2,8,256]{3,2,1,0:T(8,128)S(1)}, f32[16,2,8,256]{3,2,1,0:T(8,128)}, u32[]{:S(2)}) copy-start(f32[16,2,8,256]{3,2,1,0:T(8,128)} %constant.14.clone.inv_ref) | copy-start | bytes 786436
  1.6 0.9 %copy-start.1 = (f32[16,2,16,128]{3,2,1,0:T(8,128)S(1)}, f32[16,2,16,128]{3,2,1,0:T(8,128)}, u32[]{:S(2)}) copy-start(f32[16,2,16,128]{3,2,1,0:T(8,128)} %constant.13.clone.fwd_ref) | copy-start | bytes 786436
  2.5 0.9 %copy-start.2 = (bf16[256,512]{1,0:T(8,128)(2,1)S(1)}, bf16[256,512]{1,0:T(8,128)(2,1)}, u32[]{:S(2)}) copy-start(bf16[256,512]{1,0:T(8,128)(2,1)} %constant.12.clone.second_ref) | copy-start | bytes 786436
  3.5 0.9 %copy-start.3 = (bf16[8,16,768]{2,1,0:T(8,128)(2,1)S(1)}, bf16[8,16,768]{2,1,0:T(8,128)(2,1)}, u32[]{:S(2)}) copy-start(bf16[8,16,768]{2,1,0:T(8,128)(2,1)} %x_ref.1) | copy-start | bytes 589828
  4.4 0.9 %copy-start.4 = (bf16[8,16,768]{2,1,0:T(8,128)(2,1)S(1)}, bf16[8,16,768]{2,1,0:T(8,128)(2,1)}, u32[]{:S(2)}) copy-start(bf16[8,16,768]{2,1,0:T(8,128)(2,1)} %cot_ref.1) | copy-start | bytes 589828
  5.3 0.9 %copy-start.5 = (bf16[8,48,256]{2,1,0:T(8,128)(2,1)S(1)}, bf16[8,48,256]{2,1,0:T(8,128)(2,1)}, u32[]{:S(2)}) copy-start(bf16[8,48,256]{2,1,0:T(8,128)(2,1)} %fr_ref.1) | copy-start | bytes 589828
  6.3 0.9 %copy-start.6 = (bf16[8,48,256]{2,1,0:T(8,128)(2,1)S(1)}, bf16[8,48,256]{2,1,0:T(8,128)(2,1)}, u32[]{:S(2)}) copy-start(bf16[8,48,256]{2,1,0:T(8,128)(2,1)} %fi_ref.1) | copy-start | bytes 589828
  7.2 0.8 copy-start.7
  8.0 0.8 copy-start.8
  8.7 0.8 copy-start.9

commit v2 on v1

--- a/solution.py
+++ b/solution.py
@@ -99,8 +99,9 @@
 
 
 def kernel(
-    x_ref, w_ref, cot_ref, fr_ref, fi_ref, first_ref, last_ref, second_ref, fwd_ref, inv_ref,
+    x_hbm, w_hbm, cot_hbm, fr_ref, fi_ref, first_hbm, last_hbm, second_hbm, fwd_ref, inv_ref,
     mixed_ref, ig_ref, fgr_ref, fgi_ref, dw_ref,
+    x_ref, w_ref, cot_ref, first_ref, last_ref, second_ref,
     xt, xrecv, ct, crecv, w9, wt, wb, fo, fm, rev, fh, tf, ti,
     xp, hx_send, hx_recv, cp, ap, bp, sp, yp, fld,
     s_send, s_recv, g_send, g_recv, y_send, y_recv, z_send, z_recv,
@@ -133,6 +134,20 @@
     def wait_bytes(ref, sem):
         pltpu.make_async_copy(ref, ref, sem).wait()
 
+    leaving, arriving = {}, {}
+
+    def under_way(which, sent, received):
+        leaving[which], arriving[which] = sent, received
+
+    def arrived(which):
+        wait_bytes(arriving.pop(which), recv_sem.at[which])
+
+    def drain():
+        for which in list(arriving):
+            arrived(which)
+        for which, ref in leaving.items():
+            wait_bytes(ref, send_sem.at[which])
+
     def tile_of(ref, peer):
         return ref.at[pl.ds(pl.multiple_of(peer * DL, DL), DL)]
 
@@ -143,7 +158,16 @@
 
         lax.fori_loop(0, DL // GR, step, 0)
 
+    x_load = pltpu.make_async_copy(x_hbm, x_ref, local_sem.at[4])
+    cot_load = pltpu.make_async_copy(cot_hbm, cot_ref, local_sem.at[5])
+    w_load = pltpu.make_async_copy(w_hbm, w_ref, local_sem.at[6])
+    x_load.start()
+    cot_load.start()
+    w_load.start()
     loads = [
+        pltpu.make_async_copy(first_hbm, first_ref, local_sem.at[7]),
+        pltpu.make_async_copy(second_hbm, second_ref, local_sem.at[8]),
+        pltpu.make_async_copy(last_hbm, last_ref, local_sem.at[9]),
         pltpu.make_async_copy(fr_ref, fo.at[0], local_sem.at[0]),
         pltpu.make_async_copy(fi_ref, fo.at[1], local_sem.at[1]),
         pltpu.make_async_copy(fwd_ref.at[col], tf, local_sem.at[2]),
@@ -170,15 +194,9 @@
             block = src_ref[:, :, 128 * i : 128 * (i + 1)].reshape(128, 128).astype(F32)
             dst[128 * i : 128 * (i + 1), :] = block.T.astype(BF16)
 
+    x_load.wait()
     turn_home(x_ref, xt)
     pl.semaphore_wait(barrier, 2 * (NP - 1))
-
-    exchange("row", row, XR, lambda p: tile_of(xt, p), tile_of(xrecv, row))
-    own_rows = pl.ds(pl.multiple_of(row * DL, DL), DL)
-    xrecv[own_rows, :] = xt[own_rows, :]
-    turn_home(cot_ref, ct)
-    exchange("row", row, CR, lambda p: tile_of(ct, p), tile_of(crecv, row))
-    crecv[own_rows, :] = ct[own_rows, :]
 
     partner = 15 - col
     extra_row = jnp.where(low_half, 4, 0)
@@ -186,7 +204,19 @@
     for part, ref in enumerate((fr_ref, fi_ref)):
         remote(ref.at[pl.ds(5, 3)], fm.at[part, pl.ds(1, 3)], FM, {"col": partner}).start()
         remote(ref.at[extra_row], fm.at[part, 0], FM, {"col": extra_to}).start()
-
+    under_way(FM, fm, fm)
+
+    exchange("row", row, XR, lambda p: tile_of(xt, p), tile_of(xrecv, row))
+    under_way(XR, xt.at[pl.ds(0, 15 * DL)], xrecv.at[pl.ds(0, 15 * DL)])
+    own_rows = pl.ds(pl.multiple_of(row * DL, DL), DL)
+    xrecv[own_rows, :] = xt[own_rows, :]
+    cot_load.wait()
+    turn_home(cot_ref, ct)
+    exchange("row", row, CR, lambda p: tile_of(ct, p), tile_of(crecv, row))
+    under_way(CR, ct.at[pl.ds(0, 15 * DL)], crecv.at[pl.ds(0, 15 * DL)])
+    crecv[own_rows, :] = ct[own_rows, :]
+
+    w_load.wait()
     w9[...] = jnp.zeros_like(w9)
     for tap in range(3):
         for stream in range(3):
@@ -222,14 +252,17 @@
 
         over_groups(body)
 
-    wait_bytes(xrecv.at[pl.ds(0, 15 * DL)], recv_sem.at[XR])
+    arrived(XR)
     x3 = xrecv.reshape(NP, DL, 128)
     planes_in(x3, xp, 2)
     hx_send[0] = xp[16].astype(BF16)
     hx_send[1] = xp[17].astype(BF16)
     remote(hx_send, hx_recv, HX, {"col": lax.rem(col + 1, NP)}).start()
-
-    wait_bytes(hx_recv, recv_sem.at[HX])
+    under_way(HX, hx_send, hx_recv)
+
+    arrived(CR)
+    planes_in(crecv.reshape(NP, DL, 128), cp, 0)
+    arrived(HX)
     for i in range(2):
         halo = hx_recv[i].astype(F32)
         back = jnp.where(lane >= 16, pltpu.roll(halo, 16, 1), pltpu.roll(halo, 17, 1))
@@ -251,10 +284,8 @@
     over_groups(streams)
     tiles_out(fld, s_send, tf)
     exchange("col", col, SS, lambda p: s_send.at[p], s_recv.at[col])
+    under_way(SS, s_send.at[pl.ds(0, 15)], s_recv.at[pl.ds(0, 15)])
     s_recv[col] = s_send[col]
-
-    wait_bytes(crecv.at[pl.ds(0, 15 * DL)], recv_sem.at[CR])
-    planes_in(crecv.reshape(NP, DL, 128), cp, 0)
 
     def gate_grad(rows):
         for i in range(NP):
@@ -263,9 +294,10 @@
     over_groups(gate_grad)
     tiles_out(fld, g_send, tf)
     exchange("col", col, GG, lambda p: g_send.at[p], g_recv.at[col])
+    under_way(GG, g_send.at[pl.ds(0, 15)], g_recv.at[pl.ds(0, 15)])
     g_recv[col] = g_send[col]
 
-    wait_bytes(fm, recv_sem.at[FM])
+    arrived(FM)
     at_row = lax.broadcasted_iota(jnp.int32, (N2, N2), 0)
     at_col = lax.broadcasted_iota(jnp.int32, (N2, N2), 1)
     reverse = jnp.where(at_row + at_col == N2 - 1, 1.0, 0.0).astype(BF16)
@@ -341,7 +373,7 @@
 
         over_groups(body)
 
-    wait_bytes(s_recv.at[pl.ds(0, 15)], recv_sem.at[SS])
+    arrived(SS)
     spectrum(s_recv)
     for slot in range(5):
         re, im = parts[slot]
@@ -353,9 +385,10 @@
         pp[im] = (s_re * f_im + s_im * f_re).astype(BF16)
     restore(y_send)
     exchange("col", col, YY, lambda p: y_send.at[p], y_recv.at[col])
+    under_way(YY, y_send.at[pl.ds(0, 15)], y_recv.at[pl.ds(0, 15)])
     y_recv[col] = y_send[col]
 
-    wait_bytes(g_recv.at[pl.ds(0, 15)], recv_sem.at[GG])
+    arrived(GG)
     spectrum(g_recv)
     for slot in range(5):
         re, im = parts[slot]
@@ -376,12 +409,15 @@
             gs_send[1, 0] = jnp.where(col == 0, grad_im, gs_send[1, 0].astype(F32)).astype(BF16)
     restore(z_send)
     exchange("col", col, ZZ, lambda p: z_send.at[p], z_recv.at[col])
+    under_way(ZZ, z_send.at[pl.ds(0, 15)], z_recv.at[pl.ds(0, 15)])
     z_recv[col] = z_send[col]
-    back_to = jnp.where(low_half, jnp.where(col == 0, 8, 16 - col), partner)
-    back_to = lax.rem(back_to, NP)
-    for part in range(2):
-        remote(gs_send.at[part, pl.ds(1, 3)], gm_recv.at[part, pl.ds(1, 3)], GM, {"col": partner}).start()
-        remote(gs_send.at[part, 0], gm_recv.at[part, 0], GM, {"col": back_to}).start()
+    def send_mirrored():
+        back_to = jnp.where(low_half, jnp.where(col == 0, 8, 16 - col), partner)
+        back_to = lax.rem(back_to, NP)
+        for part in range(2):
+            remote(gs_send.at[part, pl.ds(1, 3)], gm_recv.at[part, pl.ds(1, 3)], GM, {"col": partner}).start()
+            remote(gs_send.at[part, 0], gm_recv.at[part, 0], GM, {"col": back_to}).start()
+        under_way(GM, gs_send, gm_recv)
 
     def field_back(recv, dst):
         def body(rows):
@@ -400,13 +436,15 @@
 
         over_groups(body)
 
-    wait_bytes(y_recv.at[pl.ds(0, 15)], recv_sem.at[YY])
+    arrived(YY)
     field_back(y_recv, yp)
     send_home(lambda i, rows: sp[i, rows, :] * yp[i, rows, :], m_send)
     exchange("row", row, MR, lambda p: m_send.at[p], tile_of(m_recv, row))
+    under_way(MR, m_send.at[pl.ds(0, 15)], m_recv.at[pl.ds(0, 15 * DL)])
     m_recv[own_rows, :] = m_send[row]
 
-    wait_bytes(z_recv.at[pl.ds(0, 15)], recv_sem.at[ZZ])
+    send_mirrored()
+    arrived(ZZ)
     field_back(z_recv, gp)
 
     def rounded(value):
@@ -448,12 +486,23 @@
 
     over_groups(stream_grads)
     remote(hg_send, hg_recv, HG, {"col": lax.rem(col + NP - 1, NP)}).start()
+    under_way(HG, hg_send, hg_recv)
     d1_send[...] = jnp.zeros_like(d1_send)
     d1_send[:, :DL] = wt[:DL, :].T * (1.0 / math.sqrt(SEQ))
     exchange("col", col, D1, lambda p: d1_send, d1_recv.at[col])
+    under_way(D1, d1_recv.at[pl.ds(0, 15)], d1_recv.at[pl.ds(0, 15)])
     d1_recv[col] = d1_send[...]
 
-    wait_bytes(hg_recv, recv_sem.at[HG])
+    arrived(D1)
+    total = d1_recv[0]
+    for i in range(1, NP):
+        total = total + d1_recv[i]
+    d2_send[...] = total
+    exchange("row", row, D2, lambda p: d2_send, d2_recv.at[row])
+    under_way(D2, d2_recv.at[pl.ds(0, 15)], d2_recv.at[pl.ds(0, 15)])
+    d2_recv[row] = total
+
+    arrived(HG)
     for i in range(2):
         halo = hg_recv[i].astype(F32)
         ahead = jnp.where(lane < 112, pltpu.roll(halo, 112, 1), pltpu.roll(halo, 111, 1))
@@ -461,9 +510,18 @@
         gp[14 + i] = gp[14 + i] + jnp.where(col == NP - 1, ahead, halo)
     send_home(lambda i, rows: gp[i, rows, :], i_send)
     exchange("row", row, IR, lambda p: i_send.at[p], tile_of(i_recv, row))
+    under_way(IR, i_send.at[pl.ds(0, 15)], i_recv.at[pl.ds(0, 15 * DL)])
     i_recv[own_rows, :] = i_send[row]
 
-    wait_bytes(gm_recv, recv_sem.at[GM])
+    def home(src, dst_ref):
+        for i in range(6):
+            block = src[128 * i : 128 * (i + 1), :].astype(F32).T
+            dst_ref[:, :, 128 * i : 128 * (i + 1)] = block.astype(BF16).reshape(8, 16, 128)
+
+    arrived(MR)
+    home(m_recv, mixed_ref)
+
+    arrived(GM)
     rev[...] = jnp.dot(
         gm_recv[...].reshape(8 * DL, N2), reverse, preferred_element_type=F32
     ).reshape(2, 4, DL, N2)
@@ -473,22 +531,7 @@
         fgr_ref[4 + i] = rev[0, i]
         fgi_ref[4 + i] = -rev[1, i]
 
-    wait_bytes(d1_recv.at[pl.ds(0, 15)], recv_sem.at[D1])
-    total = d1_recv[0]
-    for i in range(1, NP):
-        total = total + d1_recv[i]
-    d2_send[...] = total
-    exchange("row", row, D2, lambda p: d2_send, d2_recv.at[row])
-    d2_recv[row] = total
-
-    def home(src, dst_ref):
-        for i in range(6):
-            block = src[128 * i : 128 * (i + 1), :].astype(F32).T
-            dst_ref[:, :, 128 * i : 128 * (i + 1)] = block.astype(BF16).reshape(8, 16, 128)
-
-    wait_bytes(m_recv.at[pl.ds(0, 15 * DL)], recv_sem.at[MR])
-    home(m_recv, mixed_ref)
-    wait_bytes(d2_recv.at[pl.ds(0, 15)], recv_sem.at[D2])
+    arrived(D2)
     spot = lax.broadcasted_iota(jnp.int32, (16, 128), 1)
     blocks = [jnp.zeros((16, 128), F32)] * 6
     for i in range(NP):
@@ -505,20 +548,22 @@
             for i in range(6):
                 at = 768 * stream + 128 * i
                 dw_ref[tap : tap + 1, at : at + 128] = blocks[i][q : q + 1, :]
-    wait_bytes(i_recv.at[pl.ds(0, 15 * DL)], recv_sem.at[IR])
+    arrived(IR)
     home(i_recv, ig_ref)
 
-    wait_bytes(xt.at[pl.ds(0, 15 * DL)], send_sem.at[XR])
-    wait_bytes(ct.at[pl.ds(0, 15 * DL)], send_sem.at[CR])
-    wait_bytes(fm, send_sem.at[FM])
-    wait_bytes(hx_send, send_sem.at[HX])
-    for ref, which in (
-        (s_send, SS), (g_send, GG), (y_send, YY), (z_send, ZZ), (m_send, MR), (i_send, IR),
-        (d1_recv, D1), (d2_recv, D2),
-    ):
-        wait_bytes(ref.at[pl.ds(0, 15)], send_sem.at[which])
-    wait_bytes(gs_send, send_sem.at[GM])
-    wait_bytes(hg_send, send_sem.at[HG])
+    drain()
+
+
+def finish(*refs):
+    count = len(refs) // 2
+    sems = refs[-1]
+    copies = [
+        pltpu.make_async_copy(refs[i], refs[count + i], sems.at[i]) for i in range(count)
+    ]
+    for copy in copies:
+        copy.start()
+    for copy in copies:
+        copy.wait()
 
 
 def per_device(sequence, conv_weights, cotangent, filter_re, filter_im):
@@ -532,18 +577,25 @@
     pair = pltpu.VMEM((2, DL, 128), BF16)
     small = pltpu.VMEM((NP, 16, 128), F32)
     one = pltpu.VMEM((16, 128), F32)
-    return pl.pallas_call(
+    shapes = (
+        jax.ShapeDtypeStruct(sequence.shape, BF16),
+        jax.ShapeDtypeStruct(sequence.shape, BF16),
+        jax.ShapeDtypeStruct(filter_re.shape, F32),
+        jax.ShapeDtypeStruct(filter_re.shape, F32),
+        jax.ShapeDtypeStruct(conv_weights.shape, F32),
+    )
+    outs = pl.pallas_call(
         kernel,
-        out_shape=(
-            jax.ShapeDtypeStruct(sequence.shape, BF16),
-            jax.ShapeDtypeStruct(sequence.shape, BF16),
-            jax.ShapeDtypeStruct(filter_re.shape, F32),
-            jax.ShapeDtypeStruct(filter_re.shape, F32),
-            jax.ShapeDtypeStruct(conv_weights.shape, F32),
-        ),
-        in_specs=[vmem, vmem, vmem, hbm, hbm, vmem, vmem, vmem, hbm, hbm],
+        out_shape=shapes,
+        in_specs=[hbm] * 10,
         out_specs=[vmem] * 5,
         scratch_shapes=[
+            pltpu.VMEM(sequence.shape, BF16),
+            pltpu.VMEM(conv_weights.shape, F32),
+            pltpu.VMEM(sequence.shape, BF16),
+            pltpu.VMEM((128, 128), BF16),
+            pltpu.VMEM((128, 128), BF16),
+            pltpu.VMEM((N2, 2 * N2), BF16),
             flat, flat, flat, flat,
             pltpu.VMEM((16, 768), F32),
             pltpu.VMEM((768, 16), F32),
@@ -571,15 +623,22 @@
             tiles, flat, tiles, flat,
             pltpu.SemaphoreType.DMA((14,)),
             pltpu.SemaphoreType.DMA((14,)),
-            pltpu.SemaphoreType.DMA((4,)),
+            pltpu.SemaphoreType.DMA((10,)),
         ],
         compiler_params=pltpu.CompilerParams(
-            collective_id=0, has_side_effects=True, vmem_limit_bytes=40 * 1024 * 1024
+            collective_id=0, has_side_effects=True, vmem_limit_bytes=56 * 1024 * 1024
         ),
     )(
         sequence, conv_weights, cotangent, filter_re, filter_im,
         first, last, second, fwd, inv,
     )
+    return pl.pallas_call(
+        finish,
+        out_shape=shapes,
+        in_specs=[vmem] * 5,
+        out_specs=[hbm] * 5,
+        scratch_shapes=[pltpu.SemaphoreType.DMA((5,))],
+    )(*outs)
 
 
 def solution(mesh):

time: 78.4 us -> 69.6 us (0.89)
  local copies, waits for them, and re-layouts: 12.3 us -> 0 us
  Pallas kernels: 65 us -> 68.6 us
    unnamed x25 -> x0, local copies, waits for them, and re-layouts: 12.3 us -> none
    pallas_call x1 -> x2, Pallas kernels: 65 us -> 68.6 us  [the longest x1 66.3 us: per_device(): pl.pallas_call(kernel, out_shape=shapes, in_specs=[hbm] * 10, out_specs=[...]
where the time goes in v2:
time: 69.6 us; the launch traced here: 69.3 us
  Pallas kernels  68.6 us (99%)
    pallas_call x1, Pallas kernels, per_device(): pl.pallas_call(kernel, out_shape=shapes, in_specs=[hbm] * 10, out_specs=[...  66.3 us
    pallas_call x1, Pallas kernels, per_device(): pl.pallas_call(finish, out_shape=shapes, in_specs=[vmem] * 5, out_specs=[...  2.33 us

profile of v2, /device:TPU:1, one launch (start us, length us, event | category | flops | bytes accessed | tf_op | source)
XLA Modules:
  0.0 69.3 jit_solution(12617365103321558351)
XLA Ops:
  0.6 66.3 %shard_map.137 = (bf16[8,16,768]{2,1,0:T(8,128)(2,1)}, bf16[8,16,768]{2,1,0:T(8,128)(2,1)}, f32[8,48,256]{2,1,0:T(8,128)}, f32[8,48,256]{2,1,0:T(8,128)}, f32[3,2304]{1,0:T(4,128)}) custom-call(bf16[8,16,768]{2,1,0:T(8,128)(2,1)} %x_hbm.1, f32[3,2304]{1,0:T(4,128)} %w_hbm.1, bf16[8,16,768]{2,1,0:T(8,128)(2,1)} %cot_hbm.1, bf16[8,48,256]{2,1,0:T(8,128)(2,1)} %fr_ref.1, ...), custom_call_target="tpu_custom_call" | custom-call | tf_op jit(solution)/shard_map/pallas_call | solution.py:587
  66.9 2.3 %shard_map.138 = (bf16[8,16,768]{2,1,0:T(8,128)(2,1)}, bf16[8,16,768]{2,1,0:T(8,128)(2,1)}, f32[8,48,256]{2,1,0:T(8,128)}, f32[8,48,256]{2,1,0:T(8,128)}, f32[3,2304]{1,0:T(4,128)}) custom-call(bf16[8,16,768]{2,1,0:T(8,128)(2,1)} %get-tuple-element.10.refs_0_, bf16[8,16,768]{2,1,0:T(8,128)(2,1)} %get-tuple-element.11.refs_1_, ...), custom_call_target="tpu_custom_call" | custom-call | tf_op jit(solution)/shard_map/pallas_call | solution.py:635

commit v3 on v2

--- a/solution.py
+++ b/solution.py
@@ -100,6 +100,7 @@
 
 def kernel(
     x_hbm, w_hbm, cot_hbm, fr_ref, fi_ref, first_hbm, last_hbm, second_hbm, fwd_ref, inv_ref,
+    mixed_hbm, ig_hbm, fgr_hbm, fgi_hbm, dw_hbm,
     mixed_ref, ig_ref, fgr_ref, fgi_ref, dw_ref,
     x_ref, w_ref, cot_ref, first_ref, last_ref, second_ref,
     xt, xrecv, ct, crecv, w9, wt, wb, fo, fm, rev, fh, tf, ti,
@@ -135,6 +136,11 @@
         pltpu.make_async_copy(ref, ref, sem).wait()
 
     leaving, arriving = {}, {}
+    stores = []
+
+    def store(src, dst):
+        stores.append(pltpu.make_async_copy(src, dst, local_sem.at[10 + len(stores)]))
+        stores[-1].start()
 
     def under_way(which, sent, received):
         leaving[which], arriving[which] = sent, received
@@ -260,6 +266,22 @@
     remote(hx_send, hx_recv, HX, {"col": lax.rem(col + 1, NP)}).start()
     under_way(HX, hx_send, hx_recv)
 
+    def streams(first, last):
+        def body(rows):
+            taps = [wb[q, rows, :] for q in range(9)]
+            behind2, behind1 = xp[first, rows, :], xp[first + 1, rows, :]
+            for i in range(first, last):
+                now = xp[i + 2, rows, :]
+                z = [taps[j] * now + taps[3 + j] * behind1 + taps[6 + j] * behind2 for j in range(3)]
+                ap[i, rows, :] = z[0]
+                bp[i, rows, :] = z[1]
+                sp[i, rows, :] = z[2]
+                fld[i, rows, :] = (z[0] * z[1]).astype(BF16)
+                behind2, behind1 = behind1, now
+
+        return body
+
+    over_groups(streams(2, NP))
     arrived(CR)
     planes_in(crecv.reshape(NP, DL, 128), cp, 0)
     arrived(HX)
@@ -269,19 +291,7 @@
         back = jnp.where(lane == 0, 0.0, back)
         xp[i] = jnp.where(col == 0, back, halo)
 
-    def streams(rows):
-        taps = [wb[q, rows, :] for q in range(9)]
-        behind2, behind1 = xp[0, rows, :], xp[1, rows, :]
-        for i in range(NP):
-            now = xp[i + 2, rows, :]
-            z = [taps[j] * now + taps[3 + j] * behind1 + taps[6 + j] * behind2 for j in range(3)]
-            ap[i, rows, :] = z[0]
-            bp[i, rows, :] = z[1]
-            sp[i, rows, :] = z[2]
-            fld[i, rows, :] = (z[0] * z[1]).astype(BF16)
-            behind2, behind1 = behind1, now
-
-    over_groups(streams)
+    over_groups(streams(0, 2))
     tiles_out(fld, s_send, tf)
     exchange("col", col, SS, lambda p: s_send.at[p], s_recv.at[col])
     under_way(SS, s_send.at[pl.ds(0, 15)], s_recv.at[pl.ds(0, 15)])
@@ -488,19 +498,12 @@
     remote(hg_send, hg_recv, HG, {"col": lax.rem(col + NP - 1, NP)}).start()
     under_way(HG, hg_send, hg_recv)
     d1_send[...] = jnp.zeros_like(d1_send)
-    d1_send[:, :DL] = wt[:DL, :].T * (1.0 / math.sqrt(SEQ))
+    terms = wt[:DL, :].T * (1.0 / math.sqrt(SEQ))
+    d1_send[:, :DL] = terms[:8]
+    d1_send[0:1, 64 : 64 + DL] = terms[8:9]
     exchange("col", col, D1, lambda p: d1_send, d1_recv.at[col])
     under_way(D1, d1_recv.at[pl.ds(0, 15)], d1_recv.at[pl.ds(0, 15)])
     d1_recv[col] = d1_send[...]
-
-    arrived(D1)
-    total = d1_recv[0]
-    for i in range(1, NP):
-        total = total + d1_recv[i]
-    d2_send[...] = total
-    exchange("row", row, D2, lambda p: d2_send, d2_recv.at[row])
-    under_way(D2, d2_recv.at[pl.ds(0, 15)], d2_recv.at[pl.ds(0, 15)])
-    d2_recv[row] = total
 
     arrived(HG)
     for i in range(2):
@@ -513,6 +516,15 @@
     under_way(IR, i_send.at[pl.ds(0, 15)], i_recv.at[pl.ds(0, 15 * DL)])
     i_recv[own_rows, :] = i_send[row]
 
+    arrived(D1)
+    total = d1_recv[0]
+    for i in range(1, NP):
+        total = total + d1_recv[i]
+    d2_send[...] = total
+    exchange("row", row, D2, lambda p: d2_send, d2_recv.at[row])
+    under_way(D2, d2_recv.at[pl.ds(0, 15)], d2_recv.at[pl.ds(0, 15)])
+    d2_recv[row] = total
+
     def home(src, dst_ref):
         for i in range(6):
             block = src[128 * i : 128 * (i + 1), :].astype(F32).T
@@ -520,6 +532,7 @@
 
     arrived(MR)
     home(m_recv, mixed_ref)
+    store(mixed_ref, mixed_hbm)
 
     arrived(GM)
     rev[...] = jnp.dot(
@@ -531,12 +544,18 @@
         fgr_ref[4 + i] = rev[0, i]
         fgi_ref[4 + i] = -rev[1, i]
 
+    store(fgr_ref, fgr_hbm)
+    store(fgi_ref, fgi_hbm)
+
     arrived(D2)
     spot = lax.broadcasted_iota(jnp.int32, (16, 128), 1)
     blocks = [jnp.zeros((16, 128), F32)] * 6
     for i in range(NP):
         block, off = divmod(DL * i, 128)
-        piece = pltpu.roll(d2_recv[i], off, 1) if off else d2_recv[i]
+        packed = d2_recv[i]
+        piece = jnp.concatenate([packed, pltpu.roll(packed, 64, 1)], 0)
+        piece = jnp.where(spot < DL, piece, 0.0)
+        piece = pltpu.roll(piece, off, 1) if off else piece
         if off + DL > 128:
             blocks[block] = blocks[block] + jnp.where(spot >= off, piece, 0.0)
             blocks[block + 1] = blocks[block + 1] + jnp.where(spot < off, piece, 0.0)
@@ -548,21 +567,27 @@
             for i in range(6):
                 at = 768 * stream + 128 * i
                 dw_ref[tap : tap + 1, at : at + 128] = blocks[i][q : q + 1, :]
+    store(dw_ref, dw_hbm)
     arrived(IR)
     home(i_recv, ig_ref)
+    store(ig_ref, ig_hbm)
+    for copy in stores:
+        copy.wait()
 
     drain()
 
 
 def finish(*refs):
-    count = len(refs) // 2
-    sems = refs[-1]
-    copies = [
-        pltpu.make_async_copy(refs[i], refs[count + i], sems.at[i]) for i in range(count)
-    ]
-    for copy in copies:
+    sources, results, held = refs[:5], refs[5:10], refs[10:15]
+    load_sem, store_sem = refs[15:]
+    loads = [pltpu.make_async_copy(sources[i], held[i], load_sem.at[i]) for i in range(5)]
+    stores = [pltpu.make_async_copy(held[i], results[i], store_sem.at[i]) for i in range(5)]
+    for load in loads:
+        load.start()
+    for load, copy in zip(loads, stores):
+        load.wait()
         copy.start()
-    for copy in copies:
+    for copy in stores:
         copy.wait()
 
 
@@ -575,8 +600,8 @@
     flat = pltpu.VMEM((NP * DL, 128), BF16)
     spec = pltpu.VMEM((2, 4, DL, N2), BF16)
     pair = pltpu.VMEM((2, DL, 128), BF16)
-    small = pltpu.VMEM((NP, 16, 128), F32)
-    one = pltpu.VMEM((16, 128), F32)
+    small = pltpu.VMEM((NP, 8, 128), F32)
+    one = pltpu.VMEM((8, 128), F32)
     shapes = (
         jax.ShapeDtypeStruct(sequence.shape, BF16),
         jax.ShapeDtypeStruct(sequence.shape, BF16),
@@ -588,8 +613,9 @@
         kernel,
         out_shape=shapes,
         in_specs=[hbm] * 10,
-        out_specs=[vmem] * 5,
+        out_specs=[hbm] * 5,
         scratch_shapes=[
+            *(pltpu.VMEM(s.shape, s.dtype) for s in shapes),
             pltpu.VMEM(sequence.shape, BF16),
             pltpu.VMEM(conv_weights.shape, F32),
             pltpu.VMEM(sequence.shape, BF16),
@@ -623,7 +649,7 @@
             tiles, flat, tiles, flat,
             pltpu.SemaphoreType.DMA((14,)),
             pltpu.SemaphoreType.DMA((14,)),
-            pltpu.SemaphoreType.DMA((10,)),
+            pltpu.SemaphoreType.DMA((15,)),
         ],
         compiler_params=pltpu.CompilerParams(
             collective_id=0, has_side_effects=True, vmem_limit_bytes=56 * 1024 * 1024
@@ -635,9 +661,13 @@
     return pl.pallas_call(
         finish,
         out_shape=shapes,
-        in_specs=[vmem] * 5,
+        in_specs=[hbm] * 5,
         out_specs=[hbm] * 5,
-        scratch_shapes=[pltpu.SemaphoreType.DMA((5,))],
+        scratch_shapes=[
+            *(pltpu.VMEM(s.shape, s.dtype) for s in shapes),
+            pltpu.SemaphoreType.DMA((5,)),
+            pltpu.SemaphoreType.DMA((5,)),
+        ],
     )(*outs)
 
 

time: 69.6 us -> 67.5 us (0.970)
  Pallas kernels: 68.6 us -> 66.7 us
    pallas_call x1, Pallas kernels: 66.3 us -> 64.6 us  [per_device(): pl.pallas_call(kernel, out_shape=shapes, in_specs=[hbm] * 10, out_specs=[...]
where the time goes in v3:
time: 67.5 us; the launch traced here: 67.4 us
  Pallas kernels  66.7 us (99%)
    pallas_call x1, Pallas kernels, per_device(): pl.pallas_call(kernel, out_shape=shapes, in_specs=[hbm] * 10, out_specs=[...  64.6 us
    pallas_call x1, Pallas kernels, per_device(): pl.pallas_call(finish, out_shape=shapes, in_specs=[hbm] * 5, out_specs=[h...  2.16 us

profile of v3, /device:TPU:1, one launch (start us, length us, event | category | flops | bytes accessed | tf_op | source)
XLA Modules:
  0.0 67.4 jit_solution(16520308501527630038)
XLA Ops:
  0.6 64.6 %shard_map.137 = (bf16[8,16,768]{2,1,0:T(8,128)(2,1)}, bf16[8,16,768]{2,1,0:T(8,128)(2,1)}, f32[8,48,256]{2,1,0:T(8,128)}, f32[8,48,256]{2,1,0:T(8,128)}, f32[3,2304]{1,0:T(4,128)}) custom-call(bf16[8,16,768]{2,1,0:T(8,128)(2,1)} %x_hbm.1, f32[3,2304]{1,0:T(4,128)} %w_hbm.1, bf16[8,16,768]{2,1,0:T(8,128)(2,1)} %cot_hbm.1, bf16[8,48,256]{2,1,0:T(8,128)(2,1)} %fr_ref.1, ...), custom_call_target="tpu_custom_call" | custom-call | tf_op jit(solution)/shard_map/pallas_call | solution.py:612
  65.2 2.2 %shard_map.138 = (bf16[8,16,768]{2,1,0:T(8,128)(2,1)}, bf16[8,16,768]{2,1,0:T(8,128)(2,1)}, f32[8,48,256]{2,1,0:T(8,128)}, f32[8,48,256]{2,1,0:T(8,128)}, f32[3,2304]{1,0:T(4,128)}) custom-call(bf16[8,16,768]{2,1,0:T(8,128)(2,1)} %get-tuple-element.10.refs_0_, bf16[8,16,768]{2,1,0:T(8,128)(2,1)} %get-tuple-element.11.refs_1_, ...), custom_call_target="tpu_custom_call" | custom-call | tf_op jit(solution)/shard_map/pallas_call | solution.py:661

commit v4 on v3

--- a/solution.py
+++ b/solution.py
@@ -162,7 +162,7 @@
             body(pl.ds(pl.multiple_of(g * GR, GR), GR))
             return carry
 
-        lax.fori_loop(0, DL // GR, step, 0)
+        lax.fori_loop(0, DL // GR, step, 0, unroll=True)
 
     x_load = pltpu.make_async_copy(x_hbm, x_ref, local_sem.at[4])
     cot_load = pltpu.make_async_copy(cot_hbm, cot_ref, local_sem.at[5])

time: 67.5 us -> 64.1 us (0.950)
  Pallas kernels: 66.7 us -> 63.3 us
    pallas_call x1, Pallas kernels: 64.6 us -> 61.1 us  [per_device(): pl.pallas_call(kernel, out_shape=shapes, in_specs=[hbm] * 10, out_specs=[...]
where the time goes in v4:
time: 64.1 us; the launch traced here: 63.9 us
  Pallas kernels  63.3 us (99%)
    pallas_call x1, Pallas kernels, per_device(): pl.pallas_call(kernel, out_shape=shapes, in_specs=[hbm] * 10, out_specs=[...  61.1 us
    pallas_call x1, Pallas kernels, per_device(): pl.pallas_call(finish, out_shape=shapes, in_specs=[hbm] * 5, out_specs=[h...  2.16 us

profile of v4, /device:TPU:1, one launch (start us, length us, event | category | flops | bytes accessed | tf_op | source)
XLA Modules:
  0.0 63.9 jit_solution(15032724018435921429)
XLA Ops:
  0.6 61.1 %shard_map.137 = (bf16[8,16,768]{2,1,0:T(8,128)(2,1)}, bf16[8,16,768]{2,1,0:T(8,128)(2,1)}, f32[8,48,256]{2,1,0:T(8,128)}, f32[8,48,256]{2,1,0:T(8,128)}, f32[3,2304]{1,0:T(4,128)}) custom-call(bf16[8,16,768]{2,1,0:T(8,128)(2,1)} %x_hbm.1, f32[3,2304]{1,0:T(4,128)} %w_hbm.1, bf16[8,16,768]{2,1,0:T(8,128)(2,1)} %cot_hbm.1, bf16[8,48,256]{2,1,0:T(8,128)(2,1)} %fr_ref.1, ...), custom_call_target="tpu_custom_call" | custom-call | tf_op jit(solution)/shard_map/pallas_call | solution.py:612
  61.8 2.2 %shard_map.138 = (bf16[8,16,768]{2,1,0:T(8,128)(2,1)}, bf16[8,16,768]{2,1,0:T(8,128)(2,1)}, f32[8,48,256]{2,1,0:T(8,128)}, f32[8,48,256]{2,1,0:T(8,128)}, f32[3,2304]{1,0:T(4,128)}) custom-call(bf16[8,16,768]{2,1,0:T(8,128)(2,1)} %get-tuple-element.10.refs_0_, bf16[8,16,768]{2,1,0:T(8,128)(2,1)} %get-tuple-element.11.refs_1_, ...), custom_call_target="tpu_custom_call" | custom-call | tf_op jit(solution)/shard_map/pallas_call | solution.py:661

commit v5 on v4

--- a/solution.py
+++ b/solution.py
@@ -98,16 +98,22 @@
 HIGH3 = ((0, 4), (1, 5), (2, 6))
 
 
+def home(src, dst_ref):
+    for i in range(6):
+        block = src[128 * i : 128 * (i + 1), :].astype(F32).T
+        dst_ref[:, :, 128 * i : 128 * (i + 1)] = block.astype(BF16).reshape(8, 16, 128)
+
+
 def kernel(
     x_hbm, w_hbm, cot_hbm, fr_ref, fi_ref, first_hbm, last_hbm, second_hbm, fwd_ref, inv_ref,
-    mixed_hbm, ig_hbm, fgr_hbm, fgi_hbm, dw_hbm,
-    mixed_ref, ig_ref, fgr_ref, fgi_ref, dw_ref,
+    mixed_hbm, i_recv, fgr_hbm, fgi_hbm, d2_recv,
+    mixed_ref, fgr_ref, fgi_ref,
     x_ref, w_ref, cot_ref, first_ref, last_ref, second_ref,
     xt, xrecv, ct, crecv, w9, wt, wb, fo, fm, rev, fh, tf, ti,
     xp, hx_send, hx_recv, cp, ap, bp, sp, yp, fld,
     s_send, s_recv, g_send, g_recv, y_send, y_recv, z_send, z_recv,
-    pp, uu, sr, si, qq, gs_send, gm_recv, gp, hg_send, hg_recv,
-    d1_send, d1_recv, d2_send, d2_recv, m_send, m_recv, i_send, i_recv,
+    pp, sr, si, qq, gs_send, gm_recv, gp, third, edge, late, hg_send, hg_recv,
+    d1_send, d1_recv, d2_send, m_send, m_recv, i_send,
     send_sem, recv_sem, local_sem,
 ):
     row = lax.axis_index("row")
@@ -344,32 +350,29 @@
         pp[8] = (middle * ti[0, 4:5, :]).astype(BF16)
         pp[9] = (-middle * ti[1, 4:5, :]).astype(BF16)
         pp[4] = jnp.where(col == 0, 0.0, middle).astype(BF16)
-        uu[...] = jnp.dot(
-            pp[...].reshape(10 * DL, N2), second_ref[...], preferred_element_type=F32
-        ).reshape(10, DL, 2 * N2)
+
+    def products(slot):
+        re, im = parts[slot]
+        both = jnp.concatenate([pp[re], pp[im]], 0)
+        out = jnp.dot(both, second_ref[...], preferred_element_type=F32)
+        return out[:DL, :N2], out[:DL, N2:], out[DL:, :N2], out[DL:, N2:]
 
     def value(slot):
-        re, im = parts[slot]
-        return (
-            uu[re, :, :N2] + uu[im, :, N2:],
-            uu[im, :, :N2] - uu[re, :, N2:],
-        )
+        re_cos, re_sin, im_cos, im_sin = products(slot)
+        return re_cos + im_sin, im_cos - re_sin
+
+    def turned_back(slot):
+        re_cos, re_sin, im_cos, im_sin = products(slot)
+        return re_cos - im_sin, im_cos + re_sin
 
     def restore(dst):
-        uu[...] = jnp.dot(
-            pp[...].reshape(10 * DL, N2), second_ref[...], preferred_element_type=F32
-        ).reshape(10, DL, 2 * N2)
         for slot in range(4):
-            re, im = parts[slot]
-            z_re = uu[re, :, :N2] - uu[im, :, N2:]
-            z_im = uu[im, :, :N2] + uu[re, :, N2:]
+            z_re, z_im = turned_back(slot)
             cos, sin = ti[0, slot : slot + 1, :], ti[1, slot : slot + 1, :]
             qq[slot] = z_re * cos - z_im * sin
             q_im = z_im * cos + z_re * sin
             if slot == 0:
-                re4, im4 = parts[4]
-                z_re4 = uu[re4, :, :N2] - uu[im4, :, N2:]
-                z_im4 = uu[im4, :, :N2] + uu[re4, :, N2:]
+                z_re4, z_im4 = turned_back(4)
                 q_im = jnp.where(col == 0, z_re4 * ti[0, 4:5, :] - z_im4 * ti[1, 4:5, :], q_im)
             qq[4 + slot] = q_im
 
@@ -453,50 +456,75 @@
     under_way(MR, m_send.at[pl.ds(0, 15)], m_recv.at[pl.ds(0, 15 * DL)])
     m_recv[own_rows, :] = m_send[row]
 
-    send_mirrored()
+    def rounded(value):
+        return value.astype(BF16).astype(F32)
+
+    def third_grads(rows):
+        taps = [wb[3 * t + 2, rows, :] for t in range(3)]
+        sums = [jnp.zeros((GR, 128), F32)] * 3
+        before1 = before2 = None
+        for i in range(NP):
+            grad = rounded(cp[i, rows, :] * yp[i, rows, :])
+            at_tap = [taps[t] * grad for t in range(3)]
+            sums = [sums[t] + xp[i + 2 - t, rows, :] * grad for t in range(3)]
+            if i == 0:
+                edge[0, rows, :] = at_tap[2]
+                first_one = at_tap[1]
+            if i == 1:
+                edge[1, rows, :] = first_one + at_tap[2]
+            if before2 is not None:
+                third[i - 2, rows, :] = before2 + at_tap[2]
+            before2 = None if before1 is None else before1 + at_tap[1]
+            before1 = at_tap[0]
+        third[14, rows, :] = before2
+        third[15, rows, :] = before1
+        for t in range(3):
+            late[t, rows, :] = sums[t]
+
+    over_groups(third_grads)
+
     arrived(ZZ)
     field_back(z_recv, gp)
 
-    def rounded(value):
-        return value.astype(BF16).astype(F32)
+    def tap_grads(i, rows):
+        gs = gp[i, rows, :]
+        grads = (rounded(gs * bp[i, rows, :]), rounded(gs * ap[i, rows, :]))
+        return grads, [
+            wb[3 * t, rows, :] * grads[0] + wb[3 * t + 1, rows, :] * grads[1] for t in range(3)
+        ]
+
+    def edge_grads(rows):
+        _, first_taps = tap_grads(0, rows)
+        _, next_taps = tap_grads(1, rows)
+        hg_send[0, rows, :] = (edge[0, rows, :] + first_taps[2]).astype(BF16)
+        hg_send[1, rows, :] = (edge[1, rows, :] + first_taps[1] + next_taps[2]).astype(BF16)
+
+    over_groups(edge_grads)
+    remote(hg_send, hg_recv, HG, {"col": lax.rem(col + NP - 1, NP)}).start()
+    under_way(HG, hg_send, hg_recv)
 
     def stream_grads(rows):
-        taps = [wb[q, rows, :] for q in range(9)]
-        sums = [jnp.zeros((GR, 128), F32)] * 9
+        sums = [jnp.zeros((GR, 128), F32)] * 6
         before1 = before2 = None
         for i in range(NP):
-            gs = gp[i, rows, :]
-            grads = (
-                rounded(gs * bp[i, rows, :]),
-                rounded(gs * ap[i, rows, :]),
-                rounded(cp[i, rows, :] * yp[i, rows, :]),
-            )
-            at_tap = [
-                taps[3 * t] * grads[0] + taps[3 * t + 1] * grads[1] + taps[3 * t + 2] * grads[2]
-                for t in range(3)
-            ]
+            grads, at_tap = tap_grads(i, rows)
             past = [xp[i + 2 - t, rows, :] for t in range(3)]
-            sums = [sums[q] + past[q // 3] * grads[q % 3] for q in range(9)]
-            if i == 0:
-                hg_send[0, rows, :] = at_tap[2].astype(BF16)
-                first_one = at_tap[1]
-            if i == 1:
-                hg_send[1, rows, :] = (first_one + at_tap[2]).astype(BF16)
+            sums = [sums[q] + past[q // 2] * grads[q % 2] for q in range(6)]
             if before2 is not None:
-                gp[i - 2, rows, :] = before2 + at_tap[2]
+                gp[i - 2, rows, :] = third[i - 2, rows, :] + before2 + at_tap[2]
             before2 = None if before1 is None else before1 + at_tap[1]
             before1 = at_tap[0]
-        gp[14, rows, :] = before2
-        gp[15, rows, :] = before1
+        gp[14, rows, :] = third[14, rows, :] + before2
+        gp[15, rows, :] = third[15, rows, :] + before1
         at = lax.broadcasted_iota(jnp.int32, (GR, 128), 1)
         total = jnp.zeros((GR, 128), F32)
         for q in range(9):
-            total = jnp.where(at == q, jnp.sum(sums[q], axis=1, keepdims=True), total)
+            tap, stream = divmod(q, 3)
+            value = late[tap, rows, :] if stream == 2 else sums[2 * tap + stream]
+            total = jnp.where(at == q, jnp.sum(value, axis=1, keepdims=True), total)
         wt[rows, :] = total[:, :16]
 
     over_groups(stream_grads)
-    remote(hg_send, hg_recv, HG, {"col": lax.rem(col + NP - 1, NP)}).start()
-    under_way(HG, hg_send, hg_recv)
     d1_send[...] = jnp.zeros_like(d1_send)
     terms = wt[:DL, :].T * (1.0 / math.sqrt(SEQ))
     d1_send[:, :DL] = terms[:8]
@@ -504,6 +532,7 @@
     exchange("col", col, D1, lambda p: d1_send, d1_recv.at[col])
     under_way(D1, d1_recv.at[pl.ds(0, 15)], d1_recv.at[pl.ds(0, 15)])
     d1_recv[col] = d1_send[...]
+    send_mirrored()
 
     arrived(HG)
     for i in range(2):
@@ -514,7 +543,7 @@
     send_home(lambda i, rows: gp[i, rows, :], i_send)
     exchange("row", row, IR, lambda p: i_send.at[p], tile_of(i_recv, row))
     under_way(IR, i_send.at[pl.ds(0, 15)], i_recv.at[pl.ds(0, 15 * DL)])
-    i_recv[own_rows, :] = i_send[row]
+    store(i_send.at[row], i_recv.at[own_rows])
 
     arrived(D1)
     total = d1_recv[0]
@@ -522,13 +551,8 @@
         total = total + d1_recv[i]
     d2_send[...] = total
     exchange("row", row, D2, lambda p: d2_send, d2_recv.at[row])
-    under_way(D2, d2_recv.at[pl.ds(0, 15)], d2_recv.at[pl.ds(0, 15)])
-    d2_recv[row] = total
-
-    def home(src, dst_ref):
-        for i in range(6):
-            block = src[128 * i : 128 * (i + 1), :].astype(F32).T
-            dst_ref[:, :, 128 * i : 128 * (i + 1)] = block.astype(BF16).reshape(8, 16, 128)
+    under_way(D2, d1_recv.at[pl.ds(0, 15)], d2_recv.at[pl.ds(0, 15)])
+    store(d2_send, d2_recv.at[row])
 
     arrived(MR)
     home(m_recv, mixed_ref)
@@ -548,6 +572,31 @@
     store(fgi_ref, fgi_hbm)
 
     arrived(D2)
+    arrived(IR)
+    for copy in stores:
+        copy.wait()
+
+    drain()
+
+
+def finish(*refs):
+    sources, results, (mixed, tiles, grad_re, grad_im, d2_recv, ig_ref, dw_ref) = (
+        refs[:5], refs[5:10], refs[10:17],
+    )
+    load_sem, store_sem = refs[17:]
+    held = (mixed, tiles, grad_re, grad_im, d2_recv)
+    ready = (mixed, ig_ref, grad_re, grad_im, dw_ref)
+    loads = [pltpu.make_async_copy(sources[i], held[i], load_sem.at[i]) for i in range(5)]
+    stores = [pltpu.make_async_copy(ready[i], results[i], store_sem.at[i]) for i in range(5)]
+    for i in (1, 4, 2, 3, 0):
+        loads[i].start()
+    loads[1].wait()
+    home(tiles, ig_ref)
+    stores[1].start()
+    for i in (2, 3, 0):
+        loads[i].wait()
+        stores[i].start()
+    loads[4].wait()
     spot = lax.broadcasted_iota(jnp.int32, (16, 128), 1)
     blocks = [jnp.zeros((16, 128), F32)] * 6
     for i in range(NP):
@@ -567,26 +616,7 @@
             for i in range(6):
                 at = 768 * stream + 128 * i
                 dw_ref[tap : tap + 1, at : at + 128] = blocks[i][q : q + 1, :]
-    store(dw_ref, dw_hbm)
-    arrived(IR)
-    home(i_recv, ig_ref)
-    store(ig_ref, ig_hbm)
-    for copy in stores:
-        copy.wait()
-
-    drain()
-
-
-def finish(*refs):
-    sources, results, held = refs[:5], refs[5:10], refs[10:15]
-    load_sem, store_sem = refs[15:]
-    loads = [pltpu.make_async_copy(sources[i], held[i], load_sem.at[i]) for i in range(5)]
-    stores = [pltpu.make_async_copy(held[i], results[i], store_sem.at[i]) for i in range(5)]
-    for load in loads:
-        load.start()
-    for load, copy in zip(loads, stores):
-        load.wait()
-        copy.start()
+    stores[4].start()
     for copy in stores:
         copy.wait()
 
@@ -609,13 +639,21 @@
         jax.ShapeDtypeStruct(filter_re.shape, F32),
         jax.ShapeDtypeStruct(conv_weights.shape, F32),
     )
+    mixed, grads, filter_re_grad, filter_im_grad, weights = shapes
+    between = (
+        mixed,
+        jax.ShapeDtypeStruct((NP * DL, 128), BF16),
+        filter_re_grad,
+        filter_im_grad,
+        jax.ShapeDtypeStruct((NP, 8, 128), F32),
+    )
     outs = pl.pallas_call(
         kernel,
-        out_shape=shapes,
+        out_shape=between,
         in_specs=[hbm] * 10,
         out_specs=[hbm] * 5,
         scratch_shapes=[
-            *(pltpu.VMEM(s.shape, s.dtype) for s in shapes),
+            *(pltpu.VMEM(s.shape, s.dtype) for s in (mixed, filter_re_grad, filter_im_grad)),
             pltpu.VMEM(sequence.shape, BF16),
             pltpu.VMEM(conv_weights.shape, F32),
             pltpu.VMEM(sequence.shape, BF16),
@@ -638,15 +676,16 @@
             tiles,
             tiles, tiles, tiles, tiles, tiles, tiles, tiles, tiles,
             pltpu.VMEM((10, DL, N2), BF16),
-            pltpu.VMEM((10, DL, 2 * N2), F32),
             pltpu.VMEM((5, DL, N2), F32),
             pltpu.VMEM((5, DL, N2), F32),
             pltpu.VMEM((8, DL, N2), F32),
             spec, spec,
-            planes,
+            planes, planes,
+            pltpu.VMEM((2, DL, 128), F32),
+            pltpu.VMEM((3, DL, 128), F32),
             pair, pair,
-            one, small, one, small,
-            tiles, flat, tiles, flat,
+            one, small, one,
+            tiles, flat, tiles,
             pltpu.SemaphoreType.DMA((14,)),
             pltpu.SemaphoreType.DMA((14,)),
             pltpu.SemaphoreType.DMA((15,)),
@@ -664,7 +703,7 @@
         in_specs=[hbm] * 5,
         out_specs=[hbm] * 5,
         scratch_shapes=[
-            *(pltpu.VMEM(s.shape, s.dtype) for s in shapes),
+            *(pltpu.VMEM(s.shape, s.dtype) for s in between + (grads, weights)),
             pltpu.SemaphoreType.DMA((5,)),
             pltpu.SemaphoreType.DMA((5,)),
         ],

time: 64.1 us -> 62.8 us (0.980)
  Pallas kernels: 63.3 us -> 62 us
    pallas_call x1, Pallas kernels: 61.1 us -> 59.8 us  [per_device(): pl.pallas_call(kernel, out_shape=between, in_specs=[hbm] * 10, out_specs=...]
where the time goes in v5:
time: 62.8 us; the launch traced here: 62.6 us
  Pallas kernels  62 us (99%)
  between operations  0.64 us (1%)
    pallas_call x1, Pallas kernels, per_device(): pl.pallas_call(kernel, out_shape=between, in_specs=[hbm] * 10, out_specs=...  59.8 us
    pallas_call x1, Pallas kernels, per_device(): pl.pallas_call(finish, out_shape=shapes, in_specs=[hbm] * 5, out_specs=[h...  2.16 us

profile of v5, /device:TPU:1, one launch (start us, length us, event | category | flops | bytes accessed | tf_op | source)
XLA Modules:
  0.0 62.6 jit_solution(944298707967019024)
XLA Ops:
  0.6 59.8 %shard_map.137 = (bf16[8,16,768]{2,1,0:T(8,128)(2,1)}, bf16[768,128]{1,0:T(8,128)(2,1)}, f32[8,48,256]{2,1,0:T(8,128)}, f32[8,48,256]{2,1,0:T(8,128)}, f32[16,8,128]{2,1,0:T(8,128)}) custom-call(bf16[8,16,768]{2,1,0:T(8,128)(2,1)} %x_hbm.1, f32[3,2304]{1,0:T(4,128)} %w_hbm.1, bf16[8,16,768]{2,1,0:T(8,128)(2,1)} %cot_hbm.1, bf16[8,48,256]{2,1,0:T(8,128)(2,1)} %fr_ref.1, ...), custom_call_target="tpu_custom_call" | custom-call | tf_op jit(solution)/shard_map/pallas_call | solution.py:650
  60.5 2.2 %shard_map.138 = (bf16[8,16,768]{2,1,0:T(8,128)(2,1)}, bf16[8,16,768]{2,1,0:T(8,128)(2,1)}, f32[8,48,256]{2,1,0:T(8,128)}, f32[8,48,256]{2,1,0:T(8,128)}, f32[3,2304]{1,0:T(4,128)}) custom-call(bf16[8,16,768]{2,1,0:T(8,128)(2,1)} %get-tuple-element.10.refs_0_, bf16[768,128]{1,0:T(8,128)(2,1)} %get-tuple-element.11.refs_1_, ...), custom_call_target="tpu_custom_call" | custom-call | tf_op jit(solution)/shard_map/pallas_call | solution.py:700

commit v6 on v5

--- a/solution.py
+++ b/solution.py
@@ -131,8 +131,9 @@
         )
 
     def exchange(axis, me, which, src_at, dst):
-        def body(step, carry):
-            peer = lax.rem(me + step, NP)
+        def body(turn, carry):
+            away = lax.div(turn, 2) * (2 * lax.rem(turn, 2) - 1)
+            peer = lax.rem(me + NP // 2 + away, NP)
             remote(src_at(peer), dst, which, {axis: peer}).start()
             return carry
 
@@ -176,6 +177,19 @@
     x_load.start()
     cot_load.start()
     w_load.start()
+    barrier = pltpu.get_barrier_semaphore()
+
+    def greet(step, carry):
+        pl.semaphore_signal(
+            barrier, inc=1, device_id={"row": lax.rem(row + step, NP)}, device_id_type=MESH
+        )
+        pl.semaphore_signal(
+            barrier, inc=1, device_id={"col": lax.rem(col + step, NP)}, device_id_type=MESH
+        )
+        return carry
+
+    lax.fori_loop(1, NP, greet, 0)
+
     loads = [
         pltpu.make_async_copy(first_hbm, first_ref, local_sem.at[7]),
         pltpu.make_async_copy(second_hbm, second_ref, local_sem.at[8]),
@@ -187,19 +201,6 @@
     ]
     for load in loads:
         load.start()
-
-    barrier = pltpu.get_barrier_semaphore()
-
-    def greet(step, carry):
-        pl.semaphore_signal(
-            barrier, inc=1, device_id={"row": lax.rem(row + step, NP)}, device_id_type=MESH
-        )
-        pl.semaphore_signal(
-            barrier, inc=1, device_id={"col": lax.rem(col + step, NP)}, device_id_type=MESH
-        )
-        return carry
-
-    lax.fori_loop(1, NP, greet, 0)
 
     def turn_home(src_ref, dst):
         for i in range(6):
@@ -288,8 +289,6 @@
         return body
 
     over_groups(streams(2, NP))
-    arrived(CR)
-    planes_in(crecv.reshape(NP, DL, 128), cp, 0)
     arrived(HX)
     for i in range(2):
         halo = hx_recv[i].astype(F32)
@@ -302,6 +301,9 @@
     exchange("col", col, SS, lambda p: s_send.at[p], s_recv.at[col])
     under_way(SS, s_send.at[pl.ds(0, 15)], s_recv.at[pl.ds(0, 15)])
     s_recv[col] = s_send[col]
+
+    arrived(CR)
+    planes_in(crecv.reshape(NP, DL, 128), cp, 0)
 
     def gate_grad(rows):
         for i in range(NP):

time: 62.8 us -> 61.9 us (0.986)
  Pallas kernels: 62 us -> 61.1 us
    pallas_call x1, Pallas kernels: 59.8 us -> 58.9 us  [per_device(): pl.pallas_call(kernel, out_shape=between, in_specs=[hbm] * 10, out_specs=...]
where the time goes in v6:
time: 61.9 us; the launch traced here: 61.7 us
  Pallas kernels  61.1 us (99%)
  between operations  0.64 us (1%)
    pallas_call x1, Pallas kernels, per_device(): pl.pallas_call(kernel, out_shape=between, in_specs=[hbm] * 10, out_specs=...  58.9 us
    pallas_call x1, Pallas kernels, per_device(): pl.pallas_call(finish, out_shape=shapes, in_specs=[hbm] * 5, out_specs=[h...  2.16 us

profile of v6, /device:TPU:1, one launch (start us, length us, event | category | flops | bytes accessed | tf_op | source)
XLA Modules:
  0.0 61.7 jit_solution(9183085122198152474)
XLA Ops:
  0.6 58.9 %shard_map.137 = (bf16[8,16,768]{2,1,0:T(8,128)(2,1)}, bf16[768,128]{1,0:T(8,128)(2,1)}, f32[8,48,256]{2,1,0:T(8,128)}, f32[8,48,256]{2,1,0:T(8,128)}, f32[16,8,128]{2,1,0:T(8,128)}) custom-call(bf16[8,16,768]{2,1,0:T(8,128)(2,1)} %x_hbm.1, f32[3,2304]{1,0:T(4,128)} %w_hbm.1, bf16[8,16,768]{2,1,0:T(8,128)(2,1)} %cot_hbm.1, bf16[8,48,256]{2,1,0:T(8,128)(2,1)} %fr_ref.1, ...), custom_call_target="tpu_custom_call" | custom-call | tf_op jit(solution)/shard_map/pallas_call | solution.py:652
  59.6 2.2 %shard_map.138 = (bf16[8,16,768]{2,1,0:T(8,128)(2,1)}, bf16[8,16,768]{2,1,0:T(8,128)(2,1)}, f32[8,48,256]{2,1,0:T(8,128)}, f32[8,48,256]{2,1,0:T(8,128)}, f32[3,2304]{1,0:T(4,128)}) custom-call(bf16[8,16,768]{2,1,0:T(8,128)(2,1)} %get-tuple-element.10.refs_0_, bf16[768,128]{1,0:T(8,128)(2,1)} %get-tuple-element.11.refs_1_, ...), custom_call_target="tpu_custom_call" | custom-call | tf_op jit(solution)/shard_map/pallas_call | solution.py:702

commit v7 on v6

--- a/solution.py
+++ b/solution.py
@@ -179,7 +179,8 @@
     w_load.start()
     barrier = pltpu.get_barrier_semaphore()
 
-    def greet(step, carry):
+    def greet(turn, carry):
+        step = NP // 2 + lax.div(turn, 2) * (2 * lax.rem(turn, 2) - 1)
         pl.semaphore_signal(
             barrier, inc=1, device_id={"row": lax.rem(row + step, NP)}, device_id_type=MESH
         )

time: 61.9 us -> 61.6 us (level)
  Pallas kernels: 61.1 us -> 60.2 us
    pallas_call x1, Pallas kernels: 58.9 us -> 58.1 us  [per_device(): pl.pallas_call(kernel, out_shape=between, in_specs=[hbm] * 10, out_specs=...]
where the time goes in v7:
time: 61.6 us; the launch traced here: 60.9 us
  Pallas kernels  60.2 us (98%)
  between operations  0.64 us (1%)
    pallas_call x1, Pallas kernels, per_device(): pl.pallas_call(kernel, out_shape=between, in_specs=[hbm] * 10, out_specs=...  58.1 us
    pallas_call x1, Pallas kernels, per_device(): pl.pallas_call(finish, out_shape=shapes, in_specs=[hbm] * 5, out_specs=[h...  2.16 us

profile of v7, /device:TPU:1, one launch (start us, length us, event | category | flops | bytes accessed | tf_op | source)
XLA Modules:
  0.0 60.9 jit_solution(8335601679699568932)
XLA Ops:
  0.6 58.1 %shard_map.137 = (bf16[8,16,768]{2,1,0:T(8,128)(2,1)}, bf16[768,128]{1,0:T(8,128)(2,1)}, f32[8,48,256]{2,1,0:T(8,128)}, f32[8,48,256]{2,1,0:T(8,128)}, f32[16,8,128]{2,1,0:T(8,128)}) custom-call(bf16[8,16,768]{2,1,0:T(8,128)(2,1)} %x_hbm.1, f32[3,2304]{1,0:T(4,128)} %w_hbm.1, bf16[8,16,768]{2,1,0:T(8,128)(2,1)} %cot_hbm.1, bf16[8,48,256]{2,1,0:T(8,128)(2,1)} %fr_ref.1, ...), custom_call_target="tpu_custom_call" | custom-call | tf_op jit(solution)/shard_map/pallas_call | solution.py:653
  58.7 2.2 %shard_map.138 = (bf16[8,16,768]{2,1,0:T(8,128)(2,1)}, bf16[8,16,768]{2,1,0:T(8,128)(2,1)}, f32[8,48,256]{2,1,0:T(8,128)}, f32[8,48,256]{2,1,0:T(8,128)}, f32[3,2304]{1,0:T(4,128)}) custom-call(bf16[8,16,768]{2,1,0:T(8,128)(2,1)} %get-tuple-element.10.refs_0_, bf16[768,128]{1,0:T(8,128)(2,1)} %get-tuple-element.11.refs_1_, ...), custom_call_target="tpu_custom_call" | custom-call | tf_op jit(solution)/shard_map/pallas_call | solution.py:703
